TPU v7x, 32 devices: a whole 2x2x4 slice. The times are simulated.
32 devices in a mesh: dp: 8 (over y, x, core), tensor: 4 (over z).
Axes of the slice: x: 2, y: 2, z: 4, core: 2. Of those that a mesh axis runs over, the one named last changes fastest.
Arguments:
- hidden_in: bfloat16 [32768, 1024], P(('dp', 'tensor')), may hold values from -6 to 6
- segment_ids: int32 [8, 4096], P('dp'), may hold values from 0 to 3, never falling along the last dimension, each value on 1 to 3072 neighbouring positions
- norm_gain: bfloat16 [1024], P(('dp', 'tensor')), may hold values from 0.099609375 to 1.8984375
- w_zx: bfloat16 [1024, 2, 2048], P('dp', None, 'tensor'), may hold values from -0.1875 to 0.1875
- w_bc: bfloat16 [1024, 256], P(('dp', 'tensor')), may hold values from -0.1875 to 0.1875
- w_dt: bfloat16 [1024, 32], P('dp', 'tensor'), may hold values from -0.1875 to 0.1875
- conv_x: float32 [5, 2048], P(None, 'tensor'), may hold values from -3 to 3
- conv_bc: float32 [5, 256], replicated, may hold values from -3 to 3
- a_log: float32 [32], P('tensor'), may hold values from 0 to 2.77
- dt_bias: float32 [32], P('tensor'), may hold values from -6.9 to -2.25
- skip_gain: float32 [32], P('tensor'), may hold values from 0.5 to 1.5
- gnorm_gain: bfloat16 [2048], P('tensor'), may hold values from 0.099609375 to 1.8984375
- w_out: bfloat16 [1024, 2048], P('dp', 'tensor'), may hold values from -0.125 to 0.125
- grad_out: bfloat16 [32768, 1024], P(('dp', 'tensor')), may hold values from -6 to 6
Outputs:
- mixed: bfloat16 [32768, 1024], P(('dp', 'tensor'))
- grad_input: float32 [32768, 1024], P(('dp', 'tensor'))
- grad_norm_gain: float32 [1024], P(('dp', 'tensor'))
- grad_w_zx: float32 [1024, 2, 2048], P('dp', None, 'tensor')
- grad_w_bc: float32 [1024, 256], P(('dp', 'tensor'))
- grad_w_dt: float32 [1024, 32], P('dp', 'tensor')
- grad_conv_x: float32 [5, 2048], P(None, 'tensor')
- grad_conv_bc: float32 [5, 256], replicated
- grad_a_log: float32 [32], P('tensor')
- grad_dt_bias: float32 [32], P('tensor')
- grad_skip_gain: float32 [32], P('tensor')
- grad_gnorm_gain: float32 [2048], P('tensor')
- grad_w_out: float32 [1024, 2048], P('dp', 'tensor')
Inputs may be any that keep to these rules, and one draw needn't show every extreme that they name: `segment_ids`: in each sequence the numbers never fall and start at 0; each document has at most 3072 positions, and one has exactly that many.
All inputs are finite; a program needn't handle non-finite values.
Results may differ from a plain program's by a relative error of at most 0.017.
Values may be sent and summed in bfloat16 or wider, within the bound.
A program may use at most 256 MiB of HBM per device.

v0:
```python
import jax
import jax.numpy as jnp
from jax import lax
from jax.sharding import PartitionSpec as P

BLOCK_LEN = 256


epsilon = 1e-05
exact_mode = lax.Precision.HIGHEST


def causal_conv(values, weights, segments):
    taps = weights.shape[0] - 1
    length = values.shape[0]
    padded = jnp.concatenate([jnp.zeros((taps - 1, values.shape[1]), values.dtype), values], axis=0)
    seg_pad = jnp.concatenate([jnp.full((taps - 1,), -1, jnp.int32), segments])
    summed = jnp.zeros_like(values) + weights[taps]
    for offset in range(taps):
        matched = seg_pad[offset : offset + length] == segments
        summed = summed + weights[offset] * jnp.where(
            matched[:, None], padded[offset : offset + length], 0.0
        )
    return summed


def block_step(running, pieces):
    carry_state, before = running
    x_blk, b_blk, c_blk, a_blk, dt_blk, s_blk = pieces
    span_len = s_blk.shape[0]
    cumulative = jnp.cumsum(a_blk, axis=0).T
    row_ids = lax.broadcasted_iota(jnp.int32, (span_len, span_len), 0)
    col_ids = lax.broadcasted_iota(jnp.int32, (span_len, span_len), 1)
    allowed = (s_blk[:, None] == s_blk[None, :]) & (row_ids >= col_ids)
    gaps = cumulative[:, :, None] - cumulative[:, None, :]
    decays = jnp.exp(jnp.where(allowed[None], gaps, -jnp.inf))
    inner_prod = jnp.dot(c_blk, b_blk.T, precision=exact_mode)
    scores = inner_prod[None] * decays * dt_blk.T[:, None, :]
    y_local = jnp.einsum("hij,jhp->ihp", scores, x_blk, precision=exact_mode)
    start_w = jnp.where((s_blk == before)[:, None], jnp.exp(cumulative.T), 0.0)
    y_carry = (
        jnp.einsum("in,hpn->ihp", c_blk, carry_state, precision=exact_mode) * start_w[:, :, None]
    )
    last_seg = s_blk[span_len - 1]
    tail_weight = (
        jnp.where(
            (s_blk == last_seg)[:, None], jnp.exp(cumulative[:, span_len - 1 :] - cumulative).T, 0.0
        )
        * dt_blk
    )
    kept_share = jnp.where(last_seg == before, jnp.exp(cumulative[:, span_len - 1]), 0.0)
    new_state = jnp.einsum("jh,jhp,jn->hpn", tail_weight, x_blk, b_blk, precision=exact_mode)
    new_state = new_state + kept_share[:, None, None] * carry_state
    return ((new_state, last_seg), y_local + y_carry)


def scan_mix(inputs_x, in_map, out_map, step_size, rates, segments, block_len):
    length, head_count = step_size.shape
    blocks = length // block_len
    x_blocks = inputs_x.reshape(blocks, block_len, head_count, -1)
    a_blocks = (step_size * rates).reshape(blocks, block_len, head_count)
    start_state = jnp.zeros((head_count, x_blocks.shape[3], in_map.shape[1]), jnp.float32)
    pieces = (
        x_blocks,
        in_map.reshape(blocks, block_len, -1),
        out_map.reshape(blocks, block_len, -1),
        a_blocks,
        step_size.reshape(blocks, block_len, head_count),
        segments.reshape(blocks, block_len),
    )
    ending, outputs = lax.scan(
        jax.checkpoint(block_step), (start_state, jnp.array(-1, jnp.int32)), pieces
    )
    return outputs.reshape(length, -1)


def ssm_mixer(
    inner_x, bc_raw, dt_raw, conv_x, conv_bc, a_log, dt_bias, skip_gain, segments, block_len
):
    inputs_x = jax.nn.silu(causal_conv(inner_x, conv_x, segments))
    state_maps = jax.nn.silu(causal_conv(bc_raw, conv_bc, segments))
    half_cols = state_maps.shape[1] // 2
    step_size = jax.nn.softplus(dt_raw + dt_bias)
    head_count = step_size.shape[1]
    scanned = scan_mix(
        inputs_x,
        state_maps[:, :half_cols],
        state_maps[:, half_cols:],
        step_size,
        -jnp.exp(a_log),
        segments,
        block_len,
    )
    direct = (inputs_x.reshape(inputs_x.shape[0], head_count, -1) * skip_gain[:, None]).reshape(
        inputs_x.shape
    )
    return scanned + direct


def contract_rows(left, right):
    return lax.dot_general(
        left, right, (((0,), (0,)), ((), ())), preferred_element_type=jnp.float32
    )


def contract_cols(left, right):
    return lax.dot_general(
        left, right, (((1,), (1,)), ((), ())), preferred_element_type=jnp.float32
    )


def spread_part(part, axis_pos, parts, rank):
    full_shape = list(part.shape)
    full_shape[axis_pos] = part.shape[axis_pos] * parts
    zeros_full = jnp.zeros(tuple(full_shape), jnp.float32)
    return lax.dynamic_update_slice_in_dim(zeros_full, part, rank * part.shape[axis_pos], axis_pos)


def body(
    hidden_in,
    segment_ids,
    norm_gain,
    w_zx,
    w_bc,
    w_dt,
    conv_x,
    conv_bc,
    a_log,
    dt_bias,
    skip_gain,
    gnorm_gain,
    w_out,
    grad_out,
):
    model_dim = hidden_in.shape[1]
    tensor_count = lax.axis_size("tensor")
    tensor_rank = lax.axis_index("tensor")
    w_zx_rows, w_dt_rows, w_out_rows = (
        lax.all_gather(w_zx, "dp", axis=0, tiled=True),
        lax.all_gather(w_dt, "dp", axis=0, tiled=True),
        lax.all_gather(w_out, "dp", axis=0, tiled=True),
    )
    w_bc_full, gain_full = (
        lax.all_gather(w_bc, ("dp", "tensor"), axis=0, tiled=True),
        lax.all_gather(norm_gain, ("dp", "tensor"), axis=0, tiled=True),
    )
    inner_loc = w_zx_rows.shape[2]
    inner_total = inner_loc * tensor_count
    hidden = hidden_in.astype(jnp.float32)
    pre_scale = lax.rsqrt(jnp.mean(hidden * hidden, -1, keepdims=True) + epsilon)
    normed_loc = (hidden * pre_scale * gain_full.astype(jnp.float32)).astype(jnp.bfloat16)
    normed_all = lax.all_gather(normed_loc, "tensor", axis=0, tiled=True)
    w_zx_flat = w_zx_rows.reshape(model_dim, 2 * inner_loc)
    zx_proj = jnp.dot(normed_all, w_zx_flat, preferred_element_type=jnp.float32)
    gate_low = zx_proj[:, :inner_loc].astype(jnp.bfloat16)
    inner_x = zx_proj[:, inner_loc:]
    bc_raw = jnp.dot(normed_all, w_bc_full, preferred_element_type=jnp.float32)
    dt_raw = jnp.dot(normed_all, w_dt_rows, preferred_element_type=jnp.float32)
    segments = segment_ids[0]

    def local_mix(inner_in, bc_in, dt_in, conv_xin, conv_bcin, a_login, dt_biasin, skip_in):
        return ssm_mixer(
            inner_in,
            bc_in,
            dt_in,
            conv_xin,
            conv_bcin,
            a_login,
            dt_biasin,
            skip_in,
            segments,
            BLOCK_LEN,
        )

    mixed_y, mix_back = jax.vjp(
        local_mix, inner_x, bc_raw, dt_raw, conv_x, conv_bc, a_log, dt_bias, skip_gain
    )
    y_low = mixed_y.astype(jnp.bfloat16)
    y_val = y_low.astype(jnp.float32)
    z_val = gate_low.astype(jnp.float32)
    sigma_z = jax.nn.sigmoid(z_val)
    gated = y_val * z_val * sigma_z
    square_sum = lax.psum(jnp.sum(gated * gated, -1), "tensor")
    gate_scale = lax.rsqrt(square_sum / inner_total + epsilon)[:, None]
    gn_gain = gnorm_gain.astype(jnp.float32)
    normed_gate = (gated * gate_scale * gn_gain).astype(jnp.bfloat16)
    branch = lax.psum_scatter(
        contract_cols(normed_gate, w_out_rows).astype(jnp.bfloat16),
        "tensor",
        scatter_dimension=0,
        tiled=True,
    ).astype(jnp.float32)
    mixed = (hidden + branch).astype(jnp.bfloat16)
    cot_all = lax.all_gather(grad_out, "tensor", axis=0, tiled=True)
    d_gate_norm = jnp.dot(cot_all, w_out_rows, preferred_element_type=jnp.float32)
    d_w_out = contract_rows(cot_all, normed_gate)
    scaled_grad = d_gate_norm * gn_gain
    cross_sum = lax.psum(jnp.sum(scaled_grad * gated, -1), "tensor")
    d_gated = gate_scale * scaled_grad - gated * gate_scale**3 * (cross_sum / inner_total)[:, None]
    d_gain_part = jnp.sum(d_gate_norm * gated * gate_scale, 0)
    dy_low = (d_gated * z_val * sigma_z).astype(jnp.bfloat16)
    dz_low = (d_gated * y_val * sigma_z * (1.0 + z_val * (1.0 - sigma_z))).astype(jnp.bfloat16)
    d_inner, d_bc, d_dt, d_conv_x, d_conv_bc, d_a_log, d_dt_bias, d_skip = mix_back(
        dy_low.astype(jnp.float32)
    )
    d_inner_low = d_inner.astype(jnp.bfloat16)
    d_zx = jnp.concatenate([dz_low, d_inner_low], axis=1)
    d_dt_low = d_dt.astype(jnp.bfloat16)
    d_w_zx = contract_rows(normed_all, d_zx).reshape(model_dim, 2, inner_loc)
    d_w_dt = contract_rows(normed_all, d_dt_low)
    term = contract_cols(d_zx, w_zx_flat) + contract_cols(d_dt_low, w_dt_rows)
    summed_terms = lax.psum_scatter(
        jnp.concatenate([term, d_bc], axis=1).astype(jnp.bfloat16),
        "tensor",
        scatter_dimension=0,
        tiled=True,
    ).astype(jnp.float32)
    d_bc_low = summed_terms[:, model_dim:].astype(jnp.bfloat16)
    d_normed = summed_terms[:, :model_dim] + contract_cols(d_bc_low, w_bc_full)
    d_w_bc = contract_rows(normed_loc, d_bc_low)
    gain_val = gain_full.astype(jnp.float32)
    pre_grad = d_normed * gain_val
    d_hidden = pre_scale * pre_grad - hidden * pre_scale**3 * jnp.mean(
        pre_grad * hidden, -1, keepdims=True
    )
    grad_input = grad_out.astype(jnp.float32) + d_hidden
    d_norm_gain = jnp.sum(d_normed * hidden * pre_scale, 0)
    g_zx, g_dt, g_out = (
        lax.psum_scatter(d_w_zx, "dp", scatter_dimension=0, tiled=True),
        lax.psum_scatter(d_w_dt, "dp", scatter_dimension=0, tiled=True),
        lax.psum_scatter(d_w_out, "dp", scatter_dimension=0, tiled=True),
    )
    g_bc, g_gain = (
        lax.psum_scatter(d_w_bc, ("dp", "tensor"), scatter_dimension=0, tiled=True),
        lax.psum_scatter(d_norm_gain, ("dp", "tensor"), scatter_dimension=0, tiled=True),
    )
    sums_all = lax.psum(
        (
            spread_part(d_conv_x, 1, tensor_count, tensor_rank),
            d_conv_bc,
            spread_part(d_a_log, 0, tensor_count, tensor_rank),
            spread_part(d_dt_bias, 0, tensor_count, tensor_rank),
            spread_part(d_skip, 0, tensor_count, tensor_rank),
            spread_part(d_gain_part, 0, tensor_count, tensor_rank),
        ),
        ("dp", "tensor"),
    )
    head_loc = d_a_log.shape[0]
    g_conv_x = lax.dynamic_slice_in_dim(sums_all[0], tensor_rank * inner_loc, inner_loc, 1)
    g_a_log = lax.dynamic_slice_in_dim(sums_all[2], tensor_rank * head_loc, head_loc, 0)
    g_dt_bias = lax.dynamic_slice_in_dim(sums_all[3], tensor_rank * head_loc, head_loc, 0)
    g_skip = lax.dynamic_slice_in_dim(sums_all[4], tensor_rank * head_loc, head_loc, 0)
    g_gnorm = lax.dynamic_slice_in_dim(sums_all[5], tensor_rank * inner_loc, inner_loc, 0)
    return (
        mixed,
        grad_input,
        g_gain,
        g_zx,
        g_bc,
        g_dt,
        g_conv_x,
        sums_all[1],
        g_a_log,
        g_dt_bias,
        g_skip,
        g_gnorm,
        g_out,
    )


def solution(mesh):
    placed = (
        P(("dp", "tensor"), None),
        P("dp", None),
        P(("dp", "tensor")),
        P("dp", None, "tensor"),
        P(("dp", "tensor"), None),
        P("dp", "tensor"),
        P(None, "tensor"),
        P(),
        P("tensor"),
        P("tensor"),
        P("tensor"),
        P("tensor"),
        P("dp", "tensor"),
        P(("dp", "tensor"), None),
    )
    return jax.shard_map(
        body,
        mesh=mesh,
        in_specs=placed,
        out_specs=(
            P(("dp", "tensor"), None),
            P(("dp", "tensor"), None),
            P(("dp", "tensor")),
            P("dp", None, "tensor"),
            P(("dp", "tensor"), None),
            P("dp", "tensor"),
            P(None, "tensor"),
            P(),
            P("tensor"),
            P("tensor"),
            P("tensor"),
            P("tensor"),
            P("dp", "tensor"),
        ),
        check_vma=False,
    )
```

profile of v0, /device:TPU:0, one launch (start us, length us, event | category | flops | bytes accessed | tf_op | source)
XLA Modules:
  0.0 1811.9 jit_solution(619544131949796825)
XLA Ops:
  8.8 42.0 %all-reduce.25 = bf16[1024]{0:T(1024)(128)(2,1)S(1)} all-reduce(bf16[1024]{0:T(1024)(128)(2,1)S(1)} %dynamic-update-slice), channel_id=1, replica_groups=mesh['dp'=8,'tensor'=4] {'dp','tensor'}, use_global_device_ids=true, to_apply=%add.25 | all-reduce | flops 1024 | bytes 4096
  60.8 9.7 all_gather.23
  70.5 88.8 %all_gather.25 = bf16[1024,256]{1,0:T(8,128)(2,1)S(1)} all-gather(bf16[32,256]{1,0:T(8,128)(2,1)S(1)} %copy-done.28), channel_id=1, replica_groups=mesh['dp'=8,'tensor'=4] {'dp','tensor'}, dimensions={0}, use_global_device_ids=true | all-gather | bytes 540672 | tf_op jit(solution)/shard_map/all_gather | solution.py:144
  161.6 56.4 %all-gather.5.cloned.1.call-done = bf16[4096,1024]{1,0:T(8,128)(2,1)} async-done(((bf16[1024,1024]{1,0:T(8,128)(2,1)}), bf16[4096,1024]{1,0:T(8,128)(2,1)}) %all-gather.5.cloned.1.call-update) | async-done | bytes 8388624 | tf_op jit(solution)/shard_map/all_gather | solution.py:152
  218.0 6.1 fusion.148
  224.1 6.0 fusion.122
  232.4 11.7 fusion.147
  244.0 4.4 slice.203
  248.4 9.6 fusion.106
  258.3 12.9 reshape.533
  271.2 12.8 copy.99
  284.0 6.4 compare_select_fusion.2
  290.4 4.2 broadcast.339.clone
  294.7 218.3 %while.46 = (s32[]{:T(128)}, f32[8,64,128]{2,1,0:T(8,128)S(1)}, s32[]{:T(128)}, f32[16,256,8,64]{1,3,2,0:T(8,128)}, f32[16,8,64,128]{3,2,1,0:T(8,128)}, /*index=...) while((s32[]{:T(128)}, f32[8,64,128]{2,1,0:T(8,128)S(1)}, ...), condition=%wide.region_4.5_spmd.clone, body=%wide.region_1.4_spmd.clone.sunk | while | flops 909255168 | bytes 5261221 | solution.py:71
  299.5 3.5 fusion.226
  313.1 3.5 fusion.226
  326.8 3.5 fusion.226
  340.4 3.5 fusion.226
  354.1 3.5 fusion.226
  367.7 3.5 fusion.226
  381.4 3.5 fusion.226
  395.0 3.5 fusion.226
  422.2 3.5 fusion.226
  435.9 3.5 fusion.226
  449.5 3.5 fusion.226
  476.7 3.5 fusion.226
  490.4 3.5 fusion.226
  504.0 3.5 fusion.226
  512.9 12.3 copy.117
  525.3 14.2 reshape.529
  539.5 14.7 multiply_reduce_fusion.11
  554.1 15.6 psum.56
  569.8 12.1 multiply_reduce_fusion.4
  581.9 16.2 psum.57
  598.1 16.9 multiply_reduce_fusion.5
  615.0 11.9 reshape.530
  626.9 12.7 copy.104
  643.4 4.2 broadcast.339
  647.6 398.4 %while.47 = (s32[]{:T(128)}, f32[8,64,128]{2,1,0:T(8,128)S(1)}, f32[16,256,8,64]{1,3,2,0:T(8,128)}, f32[16,256,128]{2,1,0:T(8,128)}, f32[16,256,128]{2,1,0:T(8,1...) while((s32[]{:T(128)}, f32[8,64,128]{2,1,0:T(8,128)S(1)}, ...), condition=%wide.region_22.23_spmd.clone, body=%wide.region_10.22_spmd.clone.sunk | while | flops 2125113856 | bytes 15377010 | solution.py:71
  1046.1 11.8 multiply_reduce_fusion.15
  1057.9 7.3 broadcast_multiply_fusion.1
  1065.2 12.3 copy.120
  1077.5 14.4 reshape.531
  1091.9 22.2 %multiply_reduce_fusion.9 = (f32[512]{0:T(512)S(1)}, f32[512]{0:T(512)S(1)}, f32[512]{0:T(512)S(1)}, f32[512]{0:T(512)S(1)}, f32[512]{0:T(512)S(1)}, /*index=5*/f32[4096,512]{1,0:T(8,128)S(1)}) fusion(f32[4096,1024]{1,0:T(8,128)} %fusion.147, f32[4096,512]{1,0:T(8,128)} %copy-done, pred[4096]{0:T(1024)(128)(4,1)S(1)} %get-tuple-element.952, ...), kind=kLoop, calls=%fused_computation.174 | loop fusion | flops 50329088 | bytes 46161920 | tf_op jit(solution)/shard_map/transpose(jvp())/reduce_sum | solution.py:21
  1114.1 9.5 broadcast_multiply_fusion
  1123.6 12.3 fusion.105
  1136.0 15.2 fusion.108
  1151.5 8.3 add_convert_fusion
  1159.8 7.3 fusion.121
  1167.1 8.7 pad_maximum_fusion
  1175.8 15.5 fusion.107
  1191.3 7.3 copy.109
  1199.3 11.7 convolution_bitcast_fusion.2
  1211.1 11.3 convolution_convert_fusion
  1222.4 5.3 fusion.129
  1227.8 124.3 %reduce-scatter.8.cloned.1.call-done = bf16[1024,1280]{1,0:T(8,128)(2,1)} async-done(((bf16[4096,1280]{1,0:T(8,128)(2,1)}), bf16[1024,1280]{1,0:T(8,128)(2,1)}) %reduce-scatter.8.cloned.1.call-update) | async-done | bytes 2621456 | tf_op jit(solution)/shard_map/reduce_scatter | solution.py:212
  1358.2 79.1 %all-reduce.31.cloned.1.call-done = f32[1024,2,512]{2,1,0:T(2,128)} async-done(((f32[1024,2,512]{2,1,0:T(2,128)}), f32[1024,2,512]{2,1,0:T(2,128)}) %all-reduce.31.cloned.1.call-update) | async-done | bytes 4194320
  1439.2 43.7 %reduce-scatter.14.cloned.1.call-done = f32[128,512]{0,1:T(8,128)} async-done(((f32[1024,512]{0,1:T(8,128)}), f32[128,512]{0,1:T(8,128)}) %reduce-scatter.14.cloned.1.call-update) | async-done | bytes 262160 | tf_op jit(solution)/shard_map/reduce_scatter | solution.py:231
  1484.7 5.3 fusion.120
  1490.0 43.7 %all-reduce.28 = (f32[1024]{0:T(1024)S(1)}, f32[5,2048]{1,0:T(8,128)S(1)}, f32[5,256]{1,0:T(8,128)}, f32[32]{0:T(128)S(1)}, f32[32]{0:T(128)S(1)}, /*index=5*/f32[32]{0:T(128)S(1)}, f32[2048]{0:T(1024)S(1)}) all-reduce(f32[1024]{0:T(1024)S(1)} %get-tuple-element.831, ...), channel_id=4, replica_groups=mesh['dp'=8,'tensor'=4] {'dp','tensor'}, use_global_device_ids=true, to_apply=%region_26.27.clone | all-reduce | flops 14688 | bytes 117504
  1537.3 93.4 %reduce-scatter.6.cloned.1.call-done = bf16[1024,1024]{1,0:T(8,128)(2,1)} async-done(((bf16[4096,1024]{1,0:T(8,128)(2,1)}), bf16[1024,1024]{1,0:T(8,128)(2,1)}) %reduce-scatter.6.cloned.1.call-update) | async-done | bytes 2097168 | tf_op jit(solution)/shard_map/reduce_scatter | solution.py:187
  1630.7 5.9 fusion.117
  1636.6 29.8 %reduce-scatter.12.cloned.1.call-done = f32[128,8]{0,1:T(8,128)} async-done(((f32[1024,8]{0,1:T(8,128)}), f32[128,8]{0,1:T(8,128)}) %reduce-scatter.12.cloned.1.call-update) | async-done | bytes 4112 | tf_op jit(solution)/shard_map/reduce_scatter | solution.py:230
  1666.4 138.1 %reduce-scatter.10.cloned.1.call-done = f32[32,256]{1,0:T(8,128)} async-done(((f32[1024,256]{1,0:T(8,128)}), f32[32,256]{1,0:T(8,128)}) %reduce-scatter.10.cloned.1.call-update) | async-done | bytes 32784 | tf_op jit(solution)/shard_map/reduce_scatter | solution.py:234
  (1133 shorter events, 556.0 us)
Async XLA Ops:
  7.2 152.1 %all-gather.7.cloned.1.call-start = ((), (), s32[]{:S(2)}) async-start(), calls=%async_computation.6 | async-start | bytes 2359296 | tf_op jit(solution)/shard_map/all_gather | solution.py:139
  7.9 210.1 %all-gather.5.cloned.1.call-start = ((), (), s32[]{:S(2)}) async-start(), calls=%async_computation.5 | async-start | bytes 10485760 | tf_op jit(solution)/shard_map/all_gather | solution.py:152
  50.8 2.7 copy-start.17
  54.1 5.0 copy-start.49
  54.1 5.0 copy-start.47
  54.1 5.1 copy-start.48
  54.1 5.2 copy-start.44
  54.1 5.2 copy-start.42
  54.1 5.3 copy-start.14
  54.1 6.6 copy-start.45
  54.2 16.3 copy-start.28
  57.7 512.0 %all-gather.9.cloned.1.call-start = ((), (), s32[]{:S(2)}) async-start(), calls=%async_computation.7 | async-start | bytes 1179648 | tf_op jit(solution)/shard_map/all_gather | solution.py:141
  58.5 511.3 %all-gather.11.cloned.1.call-start = ((), (), s32[]{:S(2)}) async-start(), calls=%async_computation.9 | async-start | bytes 10485760 | tf_op jit(solution)/shard_map/all_gather | solution.py:194
  59.0 1293.1 %reduce-scatter.8.cloned.1.call-start = ((), (), s32[]{:S(2)}) async-start(), calls=%async_computation.10 | async-start | bytes 13107200 | tf_op jit(solution)/shard_map/reduce_scatter | solution.py:212
  59.1 224.9 %copy-start.40 = (f32[8]{0:T(128)}, f32[8]{0:T(128)S(1)}, u32[]{:S(2)}) copy-start(f32[8]{0:T(128)S(1)} %exponential_negate_fusion) | copy-start | bytes 100
  59.2 539.0 %copy-start.38 = (f32[512]{0:T(512)}, f32[512]{0:T(512)S(1)}, u32[]{:S(2)}) copy-start(f32[512]{0:T(512)S(1)} %convert_element_type.60) | copy-start | bytes 6148
  59.4 164.7 %copy-start.29 = (f32[1,256]{1,0:T(1,128)}, f32[1,256]{1,0:T(1,128)S(1)}, u32[]{:S(2)}) copy-start(f32[1,256]{1,0:T(1,128)S(1)} %get-tuple-element.955) | copy-start | bytes 3076
  59.4 164.7 %copy-start.31 = (f32[1,256]{1,0:T(1,128)}, f32[1,256]{1,0:T(1,128)S(1)}, u32[]{:S(2)}) copy-start(f32[1,256]{1,0:T(1,128)S(1)} %get-tuple-element.956) | copy-start | bytes 3076
  59.4 164.7 %copy-start.33 = (f32[1,256]{1,0:T(1,128)}, f32[1,256]{1,0:T(1,128)S(1)}, u32[]{:S(2)}) copy-start(f32[1,256]{1,0:T(1,128)S(1)} %get-tuple-element.957) | copy-start | bytes 3076
  59.4 164.7 %copy-start.35 = (f32[1,256]{1,0:T(1,128)}, f32[1,256]{1,0:T(1,128)S(1)}, u32[]{:S(2)}) copy-start(f32[1,256]{1,0:T(1,128)S(1)} %get-tuple-element.958) | copy-start | bytes 3076
  59.4 189.0 %copy-start.19 = (f32[1,512]{1,0:T(1,128)}, f32[1,512]{1,0:T(1,128)S(1)}, u32[]{:S(2)}) copy-start(f32[1,512]{1,0:T(1,128)S(1)} %get-tuple-element.947) | copy-start | bytes 6148
  59.4 189.0 %copy-start.21 = (f32[1,512]{1,0:T(1,128)}, f32[1,512]{1,0:T(1,128)S(1)}, u32[]{:S(2)}) copy-start(f32[1,512]{1,0:T(1,128)S(1)} %get-tuple-element.948) | copy-start | bytes 6148
  59.4 189.0 %copy-start.23 = (f32[1,512]{1,0:T(1,128)}, f32[1,512]{1,0:T(1,128)S(1)}, u32[]{:S(2)}) copy-start(f32[1,512]{1,0:T(1,128)S(1)} %get-tuple-element.949) | copy-start | bytes 6148
  59.4 189.0 %copy-start.25 = (f32[1,512]{1,0:T(1,128)}, f32[1,512]{1,0:T(1,128)S(1)}, u32[]{:S(2)}) copy-start(f32[1,512]{1,0:T(1,128)S(1)} %get-tuple-element.950) | copy-start | bytes 6148
  70.5 213.6 %copy-start.10 = (bf16[1024,8]{0,1:T(8,128)(2,1)}, bf16[1024,8]{0,1:T(8,128)(2,1)S(1)}, u32[]{:S(2)}) copy-start(bf16[1024,8]{0,1:T(8,128)(2,1)S(1)} %all_gather.23) | copy-start | bytes 49156
  159.2 64.8 %copy-start.7 = (bf16[1024,256]{1,0:T(8,128)(2,1)}, bf16[1024,256]{1,0:T(8,128)(2,1)S(1)}, u32[]{:S(2)}) copy-start(bf16[1024,256]{1,0:T(8,128)(2,1)S(1)} %all_gather.25) | copy-start | bytes 1572868
  161.6 70.8 %copy-start.5 = (bf16[128,8,2,512]{3,1,2,0:T(8,128)(2,1)}, bf16[128,8,2,512]{3,1,2,0:T(8,128)(2,1)S(1)}, u32[]{:S(2)}) copy-start(bf16[128,8,2,512]{3,1,2,0:T(8,128)(2,1)S(1)} %copy.125) | copy-start | bytes 6291460
  218.0 14.4 slice-start
  224.0 6.1 copy-start.2
  224.1 8.3 slice-start.1
  248.4 10.0 copy-start
  271.2 12.8 copy-start.43
  569.7 28.4 %copy-start.12 = (f32[4096]{0:T(1024)}, f32[4096]{0:T(1024)S(1)}, u32[]{:S(2)}) copy-start(f32[4096]{0:T(1024)S(1)} %get-tuple-element.945) | copy-start | bytes 49156
  1046.0 11.8 copy-start.30
  1046.0 11.8 copy-start.32
  1046.1 11.8 copy-start.34
  1046.1 11.9 copy-start.36
  1091.9 22.2 %copy-start.20 = (f32[1,512]{1,0:T(1,128)S(1)}, f32[1,512]{1,0:T(1,128)}, u32[]{:S(2)}) copy-start(f32[1,512]{1,0:T(1,128)} %copy-done.19) | copy-start | bytes 6148
  1091.9 22.2 %copy-start.22 = (f32[1,512]{1,0:T(1,128)S(1)}, f32[1,512]{1,0:T(1,128)}, u32[]{:S(2)}) copy-start(f32[1,512]{1,0:T(1,128)} %copy-done.21) | copy-start | bytes 6148
  1091.9 22.2 %copy-start.24 = (f32[1,512]{1,0:T(1,128)S(1)}, f32[1,512]{1,0:T(1,128)}, u32[]{:S(2)}) copy-start(f32[1,512]{1,0:T(1,128)} %copy-done.23) | copy-start | bytes 6148
  1091.9 22.2 %copy-start.26 = (f32[1,512]{1,0:T(1,128)S(1)}, f32[1,512]{1,0:T(1,128)}, u32[]{:S(2)}) copy-start(f32[1,512]{1,0:T(1,128)} %copy-done.25) | copy-start | bytes 6148
  1123.6 12.3 copy-start.4
  1135.9 15.3 copy-start.6
  1135.9 15.3 copy-start.9
  1136.0 15.3 copy-start.41
  1136.0 15.5 copy-start.11
  1151.5 8.3 copy-start.3
  1175.8 261.6 %all-reduce.31.cloned.1.call-start = ((), (), s32[]{:S(2)}) async-start(), calls=%async_computation.14 | async-start | bytes 8388608
  1198.6 0.7 copy-start.13
  1198.6 0.7 copy-start.39
  1198.6 12.5 copy-start.51
  1198.6 284.3 %reduce-scatter.14.cloned.1.call-start = ((), (), s32[]{:S(2)}) async-start(), calls=%async_computation.13 | async-start | bytes 2359296 | tf_op jit(solution)/shard_map/reduce_scatter | solution.py:231
  1211.0 419.7 %reduce-scatter.6.cloned.1.call-start = ((), (), s32[]{:S(2)}) async-start(), calls=%async_computation.8 | async-start | bytes 10485760 | tf_op jit(solution)/shard_map/reduce_scatter | solution.py:187
  1222.4 444.1 %reduce-scatter.12.cloned.1.call-start = ((), (), s32[]{:S(2)}) async-start(), calls=%async_computation.12 | async-start | bytes 36864 | tf_op jit(solution)/shard_map/reduce_scatter | solution.py:230
  1227.7 127.8 %copy-start.52 = (u32[32]{0:T(128)S(1)}, u32[32]{0:T(128)}, u32[]{:S(2)}) copy-start(u32[32]{0:T(128)} %constant.237) | copy-start | bytes 388
  1227.7 129.1 %copy-start.37 = (f32[512]{0:T(512)S(1)}, f32[512]{0:T(512)}, u32[]{:S(2)}) copy-start(f32[512]{0:T(512)} %get-tuple-element.901) | copy-start | bytes 6148
  1227.7 129.7 %copy-start.46 = (f32[512]{0:T(512)S(1)}, f32[512]{0:T(512)}, u32[]{:S(2)}) copy-start(f32[512]{0:T(512)} %get-tuple-element.817) | copy-start | bytes 6148
  1227.7 130.1 %copy-start.50 = (f32[8]{0:T(128)S(1)}, f32[8]{0:T(128)}, u32[]{:S(2)}) copy-start(f32[8]{0:T(128)} %param.26) | copy-start | bytes 100
  1227.7 257.0 %copy-start.1 = (bf16[1024,1024]{1,0:T(8,128)(2,1)S(1)}, bf16[1024,1024]{1,0:T(8,128)(2,1)}, u32[]{:S(2)}) copy-start(bf16[1024,1024]{1,0:T(8,128)(2,1)} %param.18) | copy-start | bytes 6291460
  1227.8 257.0 %copy-start.8 = (bf16[1024,256]{1,0:T(8,128)(2,1)S(1)}, bf16[1024,256]{1,0:T(8,128)(2,1)}, u32[]{:S(2)}) copy-start(bf16[1024,256]{1,0:T(8,128)(2,1)} %copy-done.7) | copy-start | bytes 1572868
  1227.8 256.9 %copy-start.16 = (f32[1024]{0:T(1024)S(1)}, f32[1024]{0:T(1024)}, u32[]{:S(2)}) copy-start(f32[1024]{0:T(1024)} %copy-done.15) | copy-start | bytes 12292
  1227.8 256.9 %copy-start.18 = (f32[1024]{0:T(1024)S(1)}, f32[1024]{0:T(1024)}, u32[]{:S(2)}) copy-start(f32[1024]{0:T(1024)} %copy-done.17) | copy-start | bytes 12292
  1227.8 576.8 %reduce-scatter.10.cloned.1.call-start = ((), (), s32[]{:S(2)}) async-start(), calls=%async_computation.11 | async-start | bytes 1081344 | tf_op jit(solution)/shard_map/reduce_scatter | solution.py:234
  1484.7 146.0 %copy-start.27 = (f32[1024]{0:T(1024)S(1)}, f32[1024]{0:T(1024)}, u32[]{:S(2)}) copy-start(f32[1024]{0:T(1024)} %get-tuple-element.959) | copy-start | bytes 12292
  (1 other events, 0.6 us)
Sparse Core Ops, SparseCore 0:
  9.9 30.7 all-gather.6
  57.8 160.0 all-gather.4
  219.9 21.9 all-gather.8
  243.3 149.6 all-gather.10
  1175.9 176.1 reduce-scatter.7
  1355.2 82.0 all-reduce.30
  1441.5 41.3 reduce-scatter.13
  1485.3 145.4 reduce-scatter.5
  1634.3 32.0 reduce-scatter.11
  1669.2 135.3 reduce-scatter.9
where the time goes:
time: 1820 us; the launch traced here: 1810 us
  waiting for transfers between devices  567 us (31%)
  matrix products  455 us (25%)
  other arithmetic  274 us (15%)
  local copies, waits for them, and re-layouts  238 us (13%)
  blocking collectives  216 us (12%)
  loops' own time  45 us (2%)
    dot_general x48, matrix products, block_step(): y_local = jnp.einsum('hij,jhp->ihp', scores, x_blk, precision=exact_mode)  154 us
    reduce_scatter x1, waiting for transfers between devices, body(): lax.psum_scatter(d_w_bc, ('dp', 'tensor'), scatter_dimension=0, tiled=True)  138 us
    reduce_scatter x1, waiting for transfers between devices, body(): lax.psum_scatter(jnp.concatenate([term, d_bc], axis=1).astype(jnp.bfloat1...  124 us
    reduce_scatter x1, waiting for transfers between devices, body(): lax.psum_scatter(contract_cols(normed_gate, w_out_rows).astype(jnp.bfloat...  93.4 us
    all_gather x1, blocking collectives, body(): lax.all_gather(w_bc, ('dp', 'tensor'), axis=0, tiled=True)  88.8 us
    unnamed x2, blocking collectives  85.7 us
    another operation x115, other arithmetic  81.5 us
    unnamed x11, waiting for transfers between devices  81.1 us
  transfers between devices with their start and end apart: 10, of which 7 were waited for; matrix products, arithmetic and copies ran while one was open for 22% of the time, Pallas kernels for 0%

commit v1 on v0

v1 whole, which is shorter than its diff:
```python
import jax
import jax.numpy as jnp
from jax import lax
from jax.experimental import pallas as pl
from jax.experimental.pallas import tpu as pltpu
from jax.sharding import PartitionSpec as P

BLOCK_LEN = 256


epsilon = 1e-05
exact_mode = lax.Precision.HIGHEST


def causal_conv(values, weights, segments):
    taps = weights.shape[0] - 1
    length = values.shape[0]
    padded = jnp.concatenate([jnp.zeros((taps - 1, values.shape[1]), values.dtype), values], axis=0)
    seg_pad = jnp.concatenate([jnp.full((taps - 1,), -1, jnp.int32), segments])
    summed = jnp.zeros_like(values) + weights[taps]
    for offset in range(taps):
        matched = seg_pad[offset : offset + length] == segments
        summed = summed + weights[offset] * jnp.where(
            matched[:, None], padded[offset : offset + length], 0.0
        )
    return summed


def exact_dot(left, right, dims):
    return lax.dot_general(
        left, right, (dims, ((), ())), precision=exact_mode, preferred_element_type=jnp.float32
    )


def low_dot(left, right, dims):
    return lax.dot_general(
        left.astype(jnp.bfloat16),
        right.astype(jnp.bfloat16),
        (dims, ((), ())),
        preferred_element_type=jnp.float32,
    )


ROWS_COLS = ((1,), (0,))
COLS_COLS = ((1,), (1,))
ROWS_ROWS = ((0,), (0,))


def block_terms(x_ref, bc_ref, cols_ref, rows_ref, rate_row_ref, rate_col_ref):
    heads = rate_row_ref.shape[1]
    span, inner = x_ref.shape
    width = inner // heads
    half = bc_ref.shape[1] // 2
    cols = cols_ref[...]
    rows = rows_ref[...]
    dt = cols[:, :heads]
    start = cols[:, heads + 1 : heads + 2]
    tail = cols[:, heads + 2 : heads + 3]
    row_ids = lax.broadcasted_iota(jnp.int32, (span, span), 0)
    col_ids = lax.broadcasted_iota(jnp.int32, (span, span), 1)
    lower = row_ids >= col_ids
    tri = jnp.where(lower, 1.0, 0.0)
    allowed = lower & (cols[:, heads : heads + 1] == rows[heads : heads + 1, :])
    cum_col = exact_dot(tri, dt * rate_row_ref[...], ROWS_COLS)
    cum_row = exact_dot(rows[:heads, :] * rate_col_ref[...], tri, COLS_COLS)
    total = cum_col[span - 1 : span, :]
    last_start = start[span - 1 : span, :]
    kept = last_start * jnp.exp(total)
    head_ids = lax.broadcasted_iota(jnp.int32, (heads, inner), 0)
    chan_ids = lax.broadcasted_iota(jnp.int32, (heads, inner), 1)
    member = jnp.where(
        (chan_ids >= head_ids * width) & (chan_ids < (head_ids + 1) * width), 1.0, 0.0
    )
    spread = exact_dot(
        jnp.concatenate([dt, start * jnp.exp(cum_col), tail * jnp.exp(total - cum_col)], axis=0),
        member,
        ROWS_COLS,
    )
    kept_wide = jnp.broadcast_to(
        last_start * jnp.exp(cum_row[:, span - 1 : span]), (heads, half)
    )
    kept_state = exact_dot(member, kept_wide, ROWS_ROWS)
    x = x_ref[...]
    dt_wide, start_wide, tail_wide = spread[:span], spread[span : 2 * span], spread[2 * span :]
    in_map = bc_ref[:, :half].astype(jnp.bfloat16)
    out_map = bc_ref[:, half:].astype(jnp.bfloat16)
    inner_prod = low_dot(out_map, in_map, COLS_COLS)

    def decay(head):
        gaps = cum_col[:, head : head + 1] - cum_row[head : head + 1, :]
        return jnp.exp(jnp.where(allowed, gaps, -jnp.inf))

    return (
        heads, width, x, x * dt_wide, dt_wide, start_wide, tail_wide,
        in_map, out_map, inner_prod, decay, kept, kept_state, member, tri,
    )


def forward_kernel(
    x_ref, bc_ref, cols_ref, rows_ref, rate_row_ref, rate_col_ref, skip_ref,
    y_ref, states_ref, state,
):
    @pl.when(pl.program_id(0) == 0)
    def _():
        state[...] = jnp.zeros_like(state)

    (heads, width, x, x_dt, dt_wide, start_wide, tail_wide,
     in_map, out_map, inner_prod, decay, kept, kept_state, member, tri) = block_terms(
        x_ref, bc_ref, cols_ref, rows_ref, rate_row_ref, rate_col_ref
    )
    before = state[...]
    states_ref[0] = before
    x_low = x_dt.astype(jnp.bfloat16)
    local = [
        low_dot(inner_prod * decay(h), x_low[:, h * width : (h + 1) * width], ROWS_COLS)
        for h in range(heads)
    ]
    y = jnp.concatenate(local, axis=1) + start_wide * low_dot(out_map, before, COLS_COLS)
    y_ref[...] = (y + skip_ref[...] * x).astype(y_ref.dtype)
    state[...] = kept_state * before + low_dot(x_dt * tail_wide, in_map, ROWS_ROWS)


def backward_kernel(
    x_ref, bc_ref, cols_ref, rows_ref, rate_row_ref, rate_col_ref, skip_ref, dy_ref, states_ref,
    dx_ref, dbc_ref, ddt_ref, da_ref, dskip_ref, dstate,
):
    @pl.when(pl.program_id(0) == 0)
    def _():
        dstate[...] = jnp.zeros_like(dstate)
        dskip_ref[...] = jnp.zeros_like(dskip_ref)

    (heads, width, x, x_dt, dt_wide, start_wide, tail_wide,
     in_map, out_map, inner_prod, decay, kept, kept_state, member, tri) = block_terms(
        x_ref, bc_ref, cols_ref, rows_ref, rate_row_ref, rate_col_ref
    )
    half = in_map.shape[1]
    before = states_ref[0]
    after_grad = dstate[...]
    dy_low = dy_ref[...]
    dy = dy_low.astype(jnp.float32)
    x_low = x_dt.astype(jnp.bfloat16)
    local, back = [], []
    d_prod = jnp.zeros_like(inner_prod)
    for h in range(heads):
        part = slice(h * width, (h + 1) * width)
        fade = decay(h)
        scores = (inner_prod * fade).astype(jnp.bfloat16)
        local.append(low_dot(scores, x_low[:, part], ROWS_COLS))
        back.append(low_dot(scores, dy_low[:, part], ROWS_ROWS))
        d_prod = d_prod + low_dot(dy_low[:, part], x_low[:, part], COLS_COLS) * fade
    dy_start = (dy * start_wide).astype(jnp.bfloat16)
    x_tail = (x_dt * tail_wide).astype(jnp.bfloat16)
    y = jnp.concatenate(local, axis=1) + start_wide * low_dot(out_map, before, COLS_COLS)
    from_state = tail_wide * low_dot(in_map, after_grad, COLS_COLS)
    local_back = jnp.concatenate(back, axis=1)
    d_xdt = local_back + from_state
    x_exact = x_low.astype(jnp.float32)
    tail_terms = from_state * x_exact
    d_cum_wide = dy * y - local_back * x_exact - tail_terms
    d_both = exact_dot(
        jnp.concatenate([d_cum_wide, d_xdt * x], axis=0), member, COLS_COLS
    )
    span = x.shape[0]
    tail_sum = jnp.sum(tail_terms, axis=0, keepdims=True)
    kept_sum = exact_dot(jnp.ones((8, half), jnp.float32), after_grad * before, COLS_COLS)
    last_both = exact_dot(
        jnp.concatenate([jnp.broadcast_to(tail_sum, kept_sum.shape), kept_sum], axis=0),
        member,
        COLS_COLS,
    )
    d_last = last_both[0:1] + kept * last_both[8:9]
    d_a = exact_dot(tri, d_both[:span], ROWS_ROWS) + d_last
    da_ref[...] = d_a
    ddt_ref[...] = d_both[span:] + d_a * rate_row_ref[...]
    dx_ref[...] = d_xdt * dt_wide + skip_ref[...] * dy
    dskip_ref[...] += jnp.broadcast_to(jnp.sum(dy * x, axis=0, keepdims=True), dskip_ref.shape)
    dbc_ref[:, :half] = low_dot(d_prod, out_map, ROWS_ROWS) + low_dot(
        x_tail, after_grad, ROWS_COLS
    )
    dbc_ref[:, half:] = low_dot(d_prod, in_map, ROWS_COLS) + low_dot(dy_start, before, ROWS_COLS)
    dstate[...] = kept_state * after_grad + low_dot(dy_start, out_map, ROWS_ROWS)


def block_specs(length, inner, maps, lanes, heads, order):
    return [
        pl.BlockSpec((BLOCK_LEN, inner), lambda i: (order(i), 0)),
        pl.BlockSpec((BLOCK_LEN, maps), lambda i: (order(i), 0)),
        pl.BlockSpec((BLOCK_LEN, lanes), lambda i: (order(i), 0)),
        pl.BlockSpec((lanes, BLOCK_LEN), lambda i: (0, order(i))),
        pl.BlockSpec((1, heads), lambda i: (0, 0)),
        pl.BlockSpec((heads, 1), lambda i: (0, 0)),
        pl.BlockSpec((1, inner), lambda i: (0, 0)),
    ]


def limits():
    return pltpu.CompilerParams(vmem_limit_bytes=48 * 1024 * 1024)


def scan_forward(xs, maps, cols, rows, rates, skip_wide):
    length, inner = xs.shape
    heads = rates.shape[0]
    half = maps.shape[1] // 2
    blocks = length // BLOCK_LEN
    return pl.pallas_call(
        forward_kernel,
        grid=(blocks,),
        in_specs=block_specs(length, inner, maps.shape[1], cols.shape[1], heads, lambda i: i),
        out_specs=[
            pl.BlockSpec((BLOCK_LEN, inner), lambda i: (i, 0)),
            pl.BlockSpec((1, inner, half), lambda i: (i, 0, 0)),
        ],
        out_shape=[
            jax.ShapeDtypeStruct((length, inner), jnp.bfloat16),
            jax.ShapeDtypeStruct((blocks, inner, half), jnp.float32),
        ],
        scratch_shapes=[pltpu.VMEM((inner, half), jnp.float32)],
        compiler_params=limits(),
        cost_estimate=pl.CostEstimate(
            flops=12 * 10**9, bytes_accessed=24 * 10**6, transcendentals=10**7
        ),
        name="scan_forward",
    )(xs, maps, cols, rows, rates[None, :], rates[:, None], skip_wide)


def scan_backward(xs, maps, cols, rows, rates, skip_wide, dy, states):
    length, inner = xs.shape
    heads = rates.shape[0]
    half = maps.shape[1] // 2
    blocks = length // BLOCK_LEN
    last = blocks - 1
    return pl.pallas_call(
        backward_kernel,
        grid=(blocks,),
        in_specs=block_specs(
            length, inner, maps.shape[1], cols.shape[1], heads, lambda i: last - i
        )
        + [
            pl.BlockSpec((BLOCK_LEN, inner), lambda i: (last - i, 0)),
            pl.BlockSpec((1, inner, half), lambda i: (last - i, 0, 0)),
        ],
        out_specs=[
            pl.BlockSpec((BLOCK_LEN, inner), lambda i: (last - i, 0)),
            pl.BlockSpec((BLOCK_LEN, 2 * half), lambda i: (last - i, 0)),
            pl.BlockSpec((BLOCK_LEN, heads), lambda i: (last - i, 0)),
            pl.BlockSpec((BLOCK_LEN, heads), lambda i: (last - i, 0)),
            pl.BlockSpec((8, inner), lambda i: (0, 0)),
        ],
        out_shape=[
            jax.ShapeDtypeStruct((length, inner), jnp.float32),
            jax.ShapeDtypeStruct((length, 2 * half), jnp.float32),
            jax.ShapeDtypeStruct((length, heads), jnp.float32),
            jax.ShapeDtypeStruct((length, heads), jnp.float32),
            jax.ShapeDtypeStruct((8, inner), jnp.float32),
        ],
        scratch_shapes=[pltpu.VMEM((inner, half), jnp.float32)],
        compiler_params=limits(),
        cost_estimate=pl.CostEstimate(
            flops=30 * 10**9, bytes_accessed=40 * 10**6, transcendentals=10**7
        ),
        name="scan_backward",
    )(xs, maps, cols, rows, rates[None, :], rates[:, None], skip_wide, dy, states)


def scan_inputs(step, segments):
    length, heads = step.shape
    ends = segments.reshape(-1, BLOCK_LEN)[:, -1]
    before = jnp.concatenate([jnp.full((1,), -1, segments.dtype), ends[:-1]])
    blocked = segments.reshape(-1, BLOCK_LEN)
    start = (blocked == before[:, None]).reshape(-1)
    tail = (blocked == ends[:, None]).reshape(-1)
    marks = jnp.stack([segments, start, tail], axis=0).astype(jnp.float32)
    extra = -(heads + 3) % 8
    rows = jnp.concatenate([step.T, marks, jnp.zeros((extra, length), jnp.float32)], axis=0)
    return rows.T, rows


def conv_parts(inner_x, bc_raw, dt_raw, conv_x, conv_bc, dt_bias, segments):
    xs = jax.nn.silu(causal_conv(inner_x, conv_x, segments))
    maps = jax.nn.silu(causal_conv(bc_raw, conv_bc, segments))
    return xs, maps, jax.nn.softplus(dt_raw + dt_bias)


def contract_rows(left, right):
    return lax.dot_general(
        left, right, (((0,), (0,)), ((), ())), preferred_element_type=jnp.float32
    )


def contract_cols(left, right):
    return lax.dot_general(
        left, right, (((1,), (1,)), ((), ())), preferred_element_type=jnp.float32
    )


def spread_part(part, axis_pos, parts, rank):
    full_shape = list(part.shape)
    full_shape[axis_pos] = part.shape[axis_pos] * parts
    zeros_full = jnp.zeros(tuple(full_shape), jnp.float32)
    return lax.dynamic_update_slice_in_dim(zeros_full, part, rank * part.shape[axis_pos], axis_pos)


def body(
    hidden_in,
    segment_ids,
    norm_gain,
    w_zx,
    w_bc,
    w_dt,
    conv_x,
    conv_bc,
    a_log,
    dt_bias,
    skip_gain,
    gnorm_gain,
    w_out,
    grad_out,
):
    model_dim = hidden_in.shape[1]
    tensor_count = lax.axis_size("tensor")
    tensor_rank = lax.axis_index("tensor")
    rows_loc = w_zx.shape[0]
    inner_loc = w_zx.shape[2]
    heads = w_dt.shape[1]
    maps_dim = w_bc.shape[1]
    inner_total = inner_loc * tensor_count
    hidden_all = lax.all_gather(hidden_in, "tensor", axis=0, tiled=True)
    few = jnp.concatenate([w_bc, jnp.pad(norm_gain[:, None], ((0, 0), (0, 127)))], axis=1)
    few_rows = lax.all_gather(few, "tensor", axis=0, tiled=True)
    w_mine = jnp.concatenate(
        [
            w_zx.reshape(rows_loc, 2 * inner_loc),
            few_rows[:, :maps_dim],
            w_dt,
            few_rows[:, maps_dim : maps_dim + 128 - heads],
        ],
        axis=1,
    )
    w_all = lax.all_gather(w_mine, "dp", axis=0, tiled=True)
    w_out_rows = lax.all_gather(w_out, "dp", axis=0, tiled=True)
    cot_all = lax.all_gather(grad_out, "tensor", axis=0, tiled=True)
    bc_at = 2 * inner_loc
    dt_at = bc_at + maps_dim
    gain_val = w_all[:, dt_at + heads].astype(jnp.float32)
    hidden = hidden_in.astype(jnp.float32)
    pre_scale = lax.rsqrt(jnp.mean(hidden * hidden, -1, keepdims=True) + epsilon)
    hidden_val = hidden_all.astype(jnp.float32)
    scale_all = lax.rsqrt(jnp.mean(hidden_val * hidden_val, -1, keepdims=True) + epsilon)
    normed_all = (hidden_val * scale_all * gain_val).astype(jnp.bfloat16)
    gate_low = jnp.dot(
        normed_all, w_all[:, :inner_loc], preferred_element_type=jnp.float32
    ).astype(jnp.bfloat16)
    inner_x = jnp.dot(
        normed_all, w_all[:, inner_loc:bc_at], preferred_element_type=jnp.float32
    )
    few_proj = jnp.dot(normed_all, w_all[:, bc_at:], preferred_element_type=jnp.float32)
    bc_raw = few_proj[:, :maps_dim]
    dt_raw = few_proj[:, maps_dim : maps_dim + heads]
    segments = segment_ids[0]

    def local_conv(inner_in, bc_in, dt_in, conv_xin, conv_bcin, dt_biasin):
        return conv_parts(inner_in, bc_in, dt_in, conv_xin, conv_bcin, dt_biasin, segments)

    (xs, maps, step), conv_back = jax.vjp(
        local_conv, inner_x, bc_raw, dt_raw, conv_x, conv_bc, dt_bias
    )
    rates = -jnp.exp(a_log)
    width = inner_loc // heads
    skip_wide = jnp.repeat(skip_gain, width)[None, :]
    cols, rows = scan_inputs(step, segments)
    y_low, states = scan_forward(xs, maps, cols, rows, rates, skip_wide)
    y_val = y_low.astype(jnp.float32)
    z_val = gate_low.astype(jnp.float32)
    sigma_z = jax.nn.sigmoid(z_val)
    gated = y_val * z_val * sigma_z
    gn_gain = gnorm_gain.astype(jnp.float32)
    d_gate_norm = jnp.dot(cot_all, w_out_rows, preferred_element_type=jnp.float32)
    scaled_grad = d_gate_norm * gn_gain
    token_sums = lax.psum(
        jnp.stack([jnp.sum(gated * gated, -1), jnp.sum(scaled_grad * gated, -1)]), "tensor"
    )
    gate_scale = lax.rsqrt(token_sums[0] / inner_total + epsilon)[:, None]
    cross_sum = token_sums[1]
    d_gated = gate_scale * scaled_grad - gated * gate_scale**3 * (cross_sum / inner_total)[:, None]
    dy_low = (d_gated * z_val * sigma_z).astype(jnp.bfloat16)
    dz_low = (d_gated * y_val * sigma_z * (1.0 + z_val * (1.0 - sigma_z))).astype(jnp.bfloat16)
    normed_gate = (gated * gate_scale * gn_gain).astype(jnp.bfloat16)
    d_gain_part = jnp.sum(d_gate_norm * gated * gate_scale, 0)
    branch = lax.psum_scatter(
        contract_cols(normed_gate, w_out_rows).astype(jnp.bfloat16),
        "tensor",
        scatter_dimension=0,
        tiled=True,
    ).astype(jnp.float32)
    mixed = (hidden + branch).astype(jnp.bfloat16)
    g_out = lax.psum_scatter(
        contract_rows(cot_all, normed_gate).astype(jnp.bfloat16),
        "dp",
        scatter_dimension=0,
        tiled=True,
    ).astype(jnp.float32)
    dxs, dmaps, dstep, d_rate_terms, dskip_rows = scan_backward(
        xs, maps, cols, rows, rates, skip_wide, dy_low, states
    )
    d_a_log = jnp.sum(d_rate_terms * step, 0) * rates
    d_skip = jnp.sum(dskip_rows[0].reshape(heads, width), 1)
    d_inner, d_bc, d_dt, d_conv_x, d_conv_bc, d_dt_bias = conv_back((dxs, dmaps, dstep))
    d_all = jnp.concatenate(
        [
            dz_low,
            d_inner.astype(jnp.bfloat16),
            d_bc.astype(jnp.bfloat16),
            d_dt.astype(jnp.bfloat16),
            jnp.zeros((d_dt.shape[0], 128 - heads), jnp.bfloat16),
        ],
        axis=1,
    )
    term = contract_cols(d_all, w_all).astype(jnp.bfloat16)
    d_normed = lax.psum_scatter(term, "tensor", scatter_dimension=0, tiled=True).astype(
        jnp.float32
    )
    d_w = contract_rows(normed_all, d_all).astype(jnp.bfloat16)
    g_all = lax.psum_scatter(d_w, "dp", scatter_dimension=0, tiled=True)
    g_bc = lax.psum_scatter(
        g_all[:, bc_at:dt_at], "tensor", scatter_dimension=0, tiled=True
    ).astype(jnp.float32)
    g_zx = g_all[:, :bc_at].astype(jnp.float32).reshape(rows_loc, 2, inner_loc)
    g_dt = g_all[:, dt_at : dt_at + heads].astype(jnp.float32)
    pre_grad = d_normed * gain_val
    d_hidden = pre_scale * pre_grad - hidden * pre_scale**3 * jnp.mean(
        pre_grad * hidden, -1, keepdims=True
    )
    grad_input = grad_out.astype(jnp.float32) + d_hidden
    d_norm_gain = jnp.sum(d_normed * hidden * pre_scale, 0)
    sums_all = lax.psum(
        (
            spread_part(d_conv_x, 1, tensor_count, tensor_rank),
            d_conv_bc,
            spread_part(d_a_log, 0, tensor_count, tensor_rank),
            spread_part(d_dt_bias, 0, tensor_count, tensor_rank),
            spread_part(d_skip, 0, tensor_count, tensor_rank),
            spread_part(d_gain_part, 0, tensor_count, tensor_rank),
            d_norm_gain,
        ),
        ("dp", "tensor"),
    )
    head_loc = d_a_log.shape[0]
    g_conv_x = lax.dynamic_slice_in_dim(sums_all[0], tensor_rank * inner_loc, inner_loc, 1)
    g_a_log = lax.dynamic_slice_in_dim(sums_all[2], tensor_rank * head_loc, head_loc, 0)
    g_dt_bias = lax.dynamic_slice_in_dim(sums_all[3], tensor_rank * head_loc, head_loc, 0)
    g_skip = lax.dynamic_slice_in_dim(sums_all[4], tensor_rank * head_loc, head_loc, 0)
    g_gnorm = lax.dynamic_slice_in_dim(sums_all[5], tensor_rank * inner_loc, inner_loc, 0)
    gain_loc = norm_gain.shape[0]
    place = lax.axis_index("dp") * tensor_count + tensor_rank
    g_gain = lax.dynamic_slice_in_dim(sums_all[6], place * gain_loc, gain_loc, 0)
    return (
        mixed,
        grad_input,
        g_gain,
        g_zx,
        g_bc,
        g_dt,
        g_conv_x,
        sums_all[1],
        g_a_log,
        g_dt_bias,
        g_skip,
        g_gnorm,
        g_out,
    )


def solution(mesh):
    placed = (
        P(("dp", "tensor"), None),
        P("dp", None),
        P(("dp", "tensor")),
        P("dp", None, "tensor"),
        P(("dp", "tensor"), None),
        P("dp", "tensor"),
        P(None, "tensor"),
        P(),
        P("tensor"),
        P("tensor"),
        P("tensor"),
        P("tensor"),
        P("dp", "tensor"),
        P(("dp", "tensor"), None),
    )
    return jax.shard_map(
        body,
        mesh=mesh,
        in_specs=placed,
        out_specs=(
            P(("dp", "tensor"), None),
            P(("dp", "tensor"), None),
            P(("dp", "tensor")),
            P("dp", None, "tensor"),
            P(("dp", "tensor"), None),
            P("dp", "tensor"),
            P(None, "tensor"),
            P(),
            P("tensor"),
            P("tensor"),
            P("tensor"),
            P("tensor"),
            P("dp", "tensor"),
        ),
        check_vma=False,
    )
```

time: 1820 us -> 1060 us (0.58)
  matrix products: 455 us -> 96.4 us
  local copies, waits for them, and re-layouts: 238 us -> 46 us
  other arithmetic: 274 us -> 114 us
  Pallas kernels: 0 us -> 143 us
  blocking collectives: 216 us -> 78.3 us
  loops' own time: 45 us -> 0 us
    dot_general x227 -> x3, matrix products: 367 us -> 28.9 us  [the longest x1 15.2 us: body(): jnp.dot(normed_all, w_all[:, :inner_loc], preferred_element_type=jnp.floa...]
    pallas_call x0 -> x2, Pallas kernels: none -> 143 us  [the longest x1 97.8 us: scan_backward(): pl.pallas_call(backward_kernel, grid=(blocks,), in_specs=block_specs(leng...]
    reduce_scatter x4 -> x3, waiting for transfers between devices: 336 us -> 193 us  [the longest x1 144 us: body(): lax.psum_scatter(term, 'tensor', scatter_dimension=0, tiled=True)]
    all_gather x3, waiting for transfers between devices: 56.4 us -> 178 us  [the longest x1 151 us: body(): hidden_all = lax.all_gather(hidden_in, 'tensor', axis=0, tiled=True)]
    unnamed x2 -> x0, blocking collectives: 85.7 us -> none
    reshape x23 -> x2, local copies, waits for them, and re-layouts: 86.5 us -> 2.4 us  [the longest x1 1.23 us: body(): g_zx = g_all[:, :bc_at].astype(jnp.float32).reshape(rows_loc, 2, inner_loc)]
    all_gather x2 -> x1, blocking collectives: 98.4 us -> 15 us  [body(): few_rows = lax.all_gather(few, 'tensor', axis=0, tiled=True)]
    all_gather x1, waiting for transfers between devices: 0.02 us -> 82.4 us  [body(): cot_all = lax.all_gather(grad_out, 'tensor', axis=0, tiled=True)]
  transfers between devices with their start and end apart: 10 -> 9, of which waited for: 7 -> 8; matrix products, arithmetic and copies ran while one was open for 22% -> 10% of each run, Pallas kernels for 0% -> 4%
where the time goes in v1:
time: 1060 us; the launch traced here: 1050 us
  waiting for transfers between devices  556 us (52%)
  Pallas kernels  143 us (13%)
  other arithmetic  114 us (11%)
  matrix products  96.4 us (9%)
  blocking collectives  78.3 us (7%)
  local copies, waits for them, and re-layouts  46 us (4%)
  between operations  14.8 us (1%)
    all_gather x1, waiting for transfers between devices, body(): hidden_all = lax.all_gather(hidden_in, 'tensor', axis=0, tiled=True)  151 us
    reduce_scatter x1, waiting for transfers between devices, body(): lax.psum_scatter(term, 'tensor', scatter_dimension=0, tiled=True)  144 us
    pallas_call x1, Pallas kernels, scan_backward(): pl.pallas_call(backward_kernel, grid=(blocks,), in_specs=block_specs(leng...  97.8 us
    reduce_scatter x1, waiting for transfers between devices, body(): lax.psum_scatter(contract_cols(normed_gate, w_out_rows).astype(jnp.bfloat...  94.9 us
    all_gather x1, waiting for transfers between devices, body(): cot_all = lax.all_gather(grad_out, 'tensor', axis=0, tiled=True)  82.4 us
    psum x1, blocking collectives, body(): lax.psum((spread_part(d_conv_x, 1, tensor_count, tensor_rank), d_conv_bc,...  46.8 us
    pallas_call x1, Pallas kernels, scan_forward(): pl.pallas_call(forward_kernel, grid=(blocks,), in_specs=block_specs(lengt...  44.7 us
    reduce_scatter x1, waiting for transfers between devices, body(): g_all = lax.psum_scatter(d_w, 'dp', scatter_dimension=0, tiled=True)  31.6 us
  transfers between devices with their start and end apart: 9, of which 8 were waited for; matrix products, arithmetic and copies ran while one was open for 10% of the time, Pallas kernels for 4%

profile of v1, /device:TPU:0, one launch (start us, length us, event | category | flops | bytes accessed | tf_op | source)
XLA Modules:
  0.0 1048.9 jit_solution(13218176611055272002)
XLA Ops:
  7.3 0.8 copy.101
  8.0 0.7 fusion.40
  8.7 15.0 %all_gather.16 = bf16[128,384]{1,0:T(8,128)(2,1)S(1)} all-gather(bf16[32,384]{1,0:T(8,128)(2,1)S(1)} %fusion.40), channel_id=1, replica_groups=mesh['dp'=8,'tensor'=4] {'tensor'}, dimensions={0}, use_global_device_ids=true | all-gather | bytes 122880 | tf_op jit(solution)/shard_map/all_gather | solution.py:329
  24.0 1.2 copy.96
  25.2 1.4 pad_maximum_fusion
  26.7 0.7 all-gather.5.cloned.1.call-update
  27.5 0.7 all-gather.11.cloned.1.call-update
  29.3 0.7 reduce.7
  31.0 0.6 copy.84
  31.8 27.8 %all-gather.7.cloned.1.call-done = bf16[1024,1408]{0,1:T(8,128)(2,1)} async-done(((bf16[128,1408]{0,1:T(8,128)(2,1)}), bf16[1024,1408]{0,1:T(8,128)(2,1)}) %all-gather.7.cloned.1.call-update) | async-done | bytes 2883600 | tf_op jit(solution)/shard_map/all_gather | solution.py:339
  59.6 0.7 slice_convert_fusion.2
  60.3 150.5 %all-gather.5.cloned.1.call-done = bf16[4096,1024]{1,0:T(8,128)(2,1)} async-done(((bf16[1024,1024]{1,0:T(8,128)(2,1)}), bf16[4096,1024]{1,0:T(8,128)(2,1)}) %all-gather.5.cloned.1.call-update) | async-done | bytes 8388624 | tf_op jit(solution)/shard_map/all_gather | solution.py:327
  210.8 5.2 fusion
  216.6 5.9 fusion.37
  222.5 2.6 slice.153
  225.1 1.2 fusion.48
  226.4 1.3 copy-done.6
  227.7 2.0 maximum_maximum_fusion
  229.7 2.2 copy.85.rows_ref
  231.8 2.4 fusion.69.cols_ref
  234.7 6.3 fusion.29
  241.0 7.9 fusion.35
  248.9 9.5 fusion.16
  258.4 44.7 %scan_forward.1 = (bf16[4096,512]{1,0:T(8,128)(2,1)}, f32[16,512,128]{2,1,0:T(8,128)}) custom-call(f32[4096,512]{1,0:T(8,128)} %get-tuple-element.109.x_ref, f32[4096,256]{1,0:T(8,128)} %get-tuple-element.107.bc_ref, f32[4096,16]{1,0:T(8,128)S(1)} %fusion.69.cols_ref, f32[16,4096]{1,0:T(8,128)S(1)} %copy.85.rows_ref, ...), custom_call_target="tpu_custom_call" | custom-call | flops 12000000000 | bytes 24000000 | tf_op jit(solution)/shard_map/scan_forward/pallas_call | solution.py:205
  303.1 82.4 %all-gather.9.cloned.1.call-done = bf16[4096,1024]{1,0:T(8,128)(2,1)} async-done(((bf16[1024,1024]{1,0:T(8,128)(2,1)}), bf16[4096,1024]{1,0:T(8,128)(2,1)}) %all-gather.9.cloned.1.call-update) | async-done | bytes 8388624 | tf_op jit(solution)/shard_map/all_gather | solution.py:341
  385.6 7.5 fusion.61
  393.1 15.2 %multiply_reduce_fusion.6 = (f32[4096]{0:T(1024)S(1)}, f32[4096]{0:T(1024)S(1)}, bf16[4096,512]{1,0:T(8,128)(2,1)}) fusion(bf16[4096,512]{1,0:T(8,128)(2,1)S(1)} %copy-done.11, f32[4096,512]{1,0:T(8,128)S(1)} %fusion.61, f32[512]{0:T(512)S(1)} %convert_element_type.106, bf16[1024,1408]{0,1:T(8,128)(2,1)} %all-gather.7.cloned.1.call-done, ...), kind=kOutput, calls=%fused_computation.38 | convolution fusion | flops 4338999296 | bytes 26269696 | tf_op jit(solution)/shard_map/dot_general | solution.py:350
  408.3 16.5 %psum.56 = f32[2,4096]{1,0:T(2,128)S(1)} all-reduce(f32[2,4096]{1,0:T(2,128)S(1)} %pad_maximum_fusion.1), channel_id=1, replica_groups=mesh['dp'=8,'tensor'=4] {'tensor'}, use_global_device_ids=true, to_apply=%region_3.4 | all-reduce | flops 8192 | bytes 65536 | tf_op jit(solution)/shard_map/psum | solution.py:379
  424.9 13.6 %fusion.14 = (bf16[4096,512]{1,0:T(8,128)(2,1)}, bf16[4096,512]{1,0:T(8,128)(2,1)}, f32[512]{0:T(512)}) fusion(bf16[4096,512]{1,0:T(8,128)(2,1)} %get-tuple-element.146, f32[4096]{0:T(1024)S(1)} %bitcast.66, f32[4096]{0:T(1024)S(1)} %multiply_multiply_fusion, f32[4096,512]{1,0:T(8,128)} %copy-done.9, f32[512]{0:T(512)S(1)} %convert_element_type.106, ...), kind=kLoop, calls=%fused_computation.22 | loop fusion | flops 52428288 | bytes 25219072 | tf_op jit(solution)/shard_map/convert_element_type | solution.py:385
  438.4 97.8 %scan_backward.1 = (f32[4096,512]{1,0:T(8,128)}, f32[4096,256]{1,0:T(8,128)}, f32[4096,8]{1,0:T(8,128)S(1)}, f32[4096,8]{1,0:T(8,128)S(1)}, f32[8,512]{1,0:T(8,128)S(1)}) custom-call(f32[4096,512]{1,0:T(8,128)} %get-tuple-element.109.x_ref, f32[4096,256]{1,0:T(8,128)} %get-tuple-element.107.bc_ref, f32[4096,16]{1,0:T(8,128)} %copy-done, ...), custom_call_target="tpu_custom_call" | custom-call | flops 30000001024 | bytes 40000000 | tf_op jit(solution)/shard_map/scan_backward/pallas_call | solution.py:232
  536.2 7.1 multiply_reduce_fusion.10
  543.4 8.5 broadcast_multiply_fusion.1
  551.9 1.8 slice-done.3
  553.7 2.4 copy-done.10
  556.1 10.4 multiply_reduce_fusion.4
  566.6 9.6 broadcast_multiply_fusion
  576.2 4.7 fusion.55
  580.9 7.1 fusion.28
  588.0 12.1 %fusion.15 = bf16[4096,512]{1,0:T(8,128)(2,1)} fusion(f32[4096,512]{1,0:T(8,128)} %get-tuple-element.115, f32[4096,512]{1,0:T(8,128)} %get-tuple-element.116, f32[4096,512]{1,0:T(8,128)} %get-tuple-element.117, f32[4096,512]{1,0:T(8,128)S(1)} %get-tuple-element.114), kind=kLoop, calls=%fused_computation.24 | loop fusion | flops 8388608 | bytes 37748736 | tf_op jit(solution)/shard_map/convert.3
  600.3 17.0 %concatenate.32 = bf16[4096,1408]{1,0:T(8,128)(2,1)} concatenate(bf16[4096,512]{1,0:T(8,128)(2,1)} %get-tuple-element.112, bf16[4096,512]{1,0:T(8,128)(2,1)} %fusion.15, bf16[4096,256]{1,0:T(8,128)(2,1)S(1)} %fusion.28, bf16[4096,8]{1,0:T(8,128)(2,1)} %get-tuple-element.104, bf16[4096,120]{1,0:T(8,128)(2,1)S(1)} %broadcast_in_dim.134), dimensions={1} | concatenate | bytes 23068672 | tf_op jit(solution)/shard_map/concatenate | solution.py:408
  617.3 19.5 %convolution_convert_fusion.3 = bf16[1024,1408]{1,0:T(8,128)(2,1)} fusion(bf16[4096,1408]{1,0:T(8,128)(2,1)} %concatenate.32, bf16[4096,1024]{1,0:T(8,128)(2,1)} %all-gather.5.cloned.1.call-done, f32[1024]{0:T(1024)S(1)} %bitcast.72, f32[4096]{0:T(1024)S(1)} %add_rsqrt_fusion), kind=kOutput, calls=%fused_computation.87 | convolution fusion | flops 11829379072 | bytes 22827008 | tf_op jit(solution)/shard_map/dot_general | solution.py:285
  637.1 10.9 %fusion.33 = bf16[1024,512]{0,1:T(8,128)(2,1)S(1)} fusion(bf16[4096,1024]{1,0:T(8,128)(2,1)} %all-gather.9.cloned.1.call-done, f32[4096]{0:T(1024)S(1)} %bitcast.64, f32[512]{0:T(512)S(1)} %convert_element_type.106, bf16[4096,512]{1,0:T(8,128)(2,1)} %get-tuple-element.146, bf16[4096,512]{1,0:T(8,128)(2,1)} %get-tuple-element.20), kind=kOutput, calls=%fused_computation.96 | convolution fusion | flops 4316463104 | bytes 17844224 | tf_op jit(solution)/shard_map/dot_general | solution.py:285
  648.0 1.3 copy.97
  649.4 31.6 %reduce-scatter.12.cloned.1.call-done = bf16[128,1408]{1,0:T(8,128)(2,1)} async-done(((bf16[1024,1408]{1,0:T(8,128)(2,1)}), bf16[128,1408]{1,0:T(8,128)(2,1)}) %reduce-scatter.12.cloned.1.call-update) | async-done | bytes 360464 | tf_op jit(solution)/shard_map/reduce_scatter | solution.py:423
  681.0 1.5 slice.161
  682.6 18.9 %convolution_convert_fusion = bf16[4096,1024]{1,0:T(8,128)(2,1)} fusion(bf16[4096,1408]{1,0:T(8,128)(2,1)} %concatenate.32, bf16[1024,1408]{0,1:T(8,128)(2,1)} %all-gather.7.cloned.1.call-done), kind=kOutput, calls=%fused_computation.50 | convolution fusion | flops 11815354368 | bytes 22806528 | tf_op jit(solution)/shard_map/dot_general | solution.py:291
  701.8 0.9 copy-done.22
  702.7 10.6 %convolution_convert_fusion.1 = bf16[4096,1024]{1,0:T(8,128)(2,1)} fusion(bf16[1024,512]{1,0:T(8,128)(2,1)S(1)} %copy-done.22, f32[4096]{0:T(1024)S(1)} %bitcast.65, f32[512]{0:T(512)S(1)} %convert_element_type.106, bf16[4096,512]{1,0:T(8,128)(2,1)} %get-tuple-element.146, bf16[4096,512]{1,0:T(8,128)(2,1)} %get-tuple-element.20), kind=kOutput, calls=%fused_computation.51 | convolution fusion | flops 4320133120 | bytes 17844224 | tf_op jit(solution)/shard_map/dot_general | solution.py:291
  713.4 1.5 copy-done.4
  716.5 4.5 reduce-scatter.16.cloned.1.call-done
  721.0 1.0 copy.98
  722.1 0.8 copy.93
  722.9 0.7 copy.92
  723.6 1.2 reshape.177
  724.8 18.1 %reduce-scatter.14.cloned.1.call-done = bf16[32,256]{1,0:T(8,128)(2,1)} async-done(((bf16[128,256]{1,0:T(8,128)(2,1)}), bf16[32,256]{1,0:T(8,128)(2,1)}) %reduce-scatter.14.cloned.1.call-update) | async-done | bytes 16400 | tf_op jit(solution)/shard_map/reduce_scatter | solution.py:424
  743.0 1.3 convert_element_type.118
  744.3 143.7 %reduce-scatter.10.cloned.1.call-done = bf16[1024,1024]{1,0:T(8,128)(2,1)} async-done(((bf16[4096,1024]{1,0:T(8,128)(2,1)}), bf16[1024,1024]{1,0:T(8,128)(2,1)}) %reduce-scatter.10.cloned.1.call-update) | async-done | bytes 2097168 | tf_op jit(solution)/shard_map/reduce_scatter | solution.py:419
  888.0 3.2 fusion.27
  891.2 46.8 %all-reduce.22 = (f32[1024]{0:T(1024)S(1)}, f32[5,2048]{1,0:T(8,128)S(1)}, f32[5,256]{1,0:T(8,128)}, f32[32]{0:T(128)S(1)}, f32[32]{0:T(128)S(1)}, /*index=5*/f32[32]{0:T(128)S(1)}, f32[2048]{0:T(1024)S(1)}) all-reduce(f32[1024]{0:T(1024)S(1)} %get-tuple-element.94, ...), channel_id=1, replica_groups=mesh['dp'=8,'tensor'=4] {'dp','tensor'}, use_global_device_ids=true, to_apply=%region_9.10 | all-reduce | flops 14688 | bytes 117504 | tf_op jit(solution)/shard_map/psum | solution.py:435
  938.0 0.6 dynamic_slice.20
  939.8 0.7 dynamic_slice.23
  941.0 0.6 constant_dynamic-slice_fusion
  941.6 94.9 %reduce-scatter.8.cloned.1.call-done = bf16[1024,1024]{1,0:T(8,128)(2,1)} async-done(((bf16[4096,1024]{1,0:T(8,128)(2,1)}), bf16[1024,1024]{1,0:T(8,128)(2,1)}) %reduce-scatter.8.cloned.1.call-update) | async-done | bytes 2097168 | tf_op jit(solution)/shard_map/reduce_scatter | solution.py:389
  1036.5 5.4 fusion.19
  (122 shorter events, 8.1 us)
Async XLA Ops:
  7.2 22.1 %copy-start.13 = (s32[1,4096]{1,0:T(1,128)S(1)}, s32[1,4096]{1,0:T(1,128)}, u32[]{:S(2)}) copy-start(s32[1,4096]{1,0:T(1,128)} %param.15) | copy-start | bytes 49156
  7.2 23.0 %copy-start.20 = (f32[8]{0:T(128)S(1)}, f32[8]{0:T(128)}, u32[]{:S(2)}) copy-start(f32[8]{0:T(128)} %param.22) | copy-start | bytes 100
  7.2 23.0 %copy-start.18 = (bf16[512]{0:T(512)(128)(2,1)S(1)}, bf16[512]{0:T(512)(128)(2,1)}, u32[]{:S(2)}) copy-start(bf16[512]{0:T(512)(128)(2,1)} %param.25) | copy-start | bytes 3076
  7.2 23.1 %copy-start.19 = (f32[8]{0:T(128)S(1)}, f32[8]{0:T(128)}, u32[]{:S(2)}) copy-start(f32[8]{0:T(128)} %param.24) | copy-start | bytes 100
  7.2 52.4 %all-gather.7.cloned.1.call-start = ((), (), s32[]{:S(2)}) async-start(), calls=%async_computation.6 | async-start | bytes 3244032 | tf_op jit(solution)/shard_map/all_gather | solution.py:339
  24.0 7.7 copy-start.16
  24.0 7.7 copy-start.15
  26.7 184.2 %all-gather.5.cloned.1.call-start = ((), (), s32[]{:S(2)}) async-start(), calls=%async_computation.5 | async-start | bytes 10485760 | tf_op jit(solution)/shard_map/all_gather | solution.py:327
  27.4 275.7 %all-gather.11.cloned.1.call-start = ((), (), s32[]{:S(2)}) async-start(), calls=%async_computation.8 | async-start | bytes 1179648 | tf_op jit(solution)/shard_map/all_gather | solution.py:340
  28.2 357.4 %all-gather.9.cloned.1.call-start = ((), (), s32[]{:S(2)}) async-start(), calls=%async_computation.7 | async-start | bytes 10485760 | tf_op jit(solution)/shard_map/all_gather | solution.py:341
  28.7 652.3 %reduce-scatter.12.cloned.1.call-start = ((), (), s32[]{:S(2)}) async-start(), calls=%async_computation.11 | async-start | bytes 3244032 | tf_op jit(solution)/shard_map/reduce_scatter | solution.py:423
  210.8 5.8 copy-start.8
  222.5 3.9 copy-start.5
  222.5 2.6 copy-start.17
  226.4 1.3 copy-start.6
  231.8 2.9 copy-start.1
  234.2 24.2 %copy-start = (f32[4096,16]{1,0:T(8,128)}, f32[4096,16]{1,0:T(8,128)S(1)}, u32[]{:S(2)}) copy-start(f32[4096,16]{1,0:T(8,128)S(1)} %fusion.69.cols_ref) | copy-start | bytes 786436
  248.9 9.5 copy-start.3
  385.6 7.5 copy-start.11
  393.1 15.2 %copy-start.9 = (f32[4096,512]{1,0:T(8,128)}, f32[4096,512]{1,0:T(8,128)S(1)}, u32[]{:S(2)}) copy-start(f32[4096,512]{1,0:T(8,128)S(1)} %fusion.61) | copy-start | bytes 25165828
  438.4 97.8 %copy-start.2 = (f32[4096,256]{1,0:T(8,128)S(1)}, f32[4096,256]{1,0:T(8,128)}, u32[]{:S(2)}) copy-start(f32[4096,256]{1,0:T(8,128)} %slice.153) | copy-start | bytes 12582916
  438.4 97.8 %copy-start.7 = (f32[4096,256]{1,0:T(8,128)S(1)}, f32[4096,256]{1,0:T(8,128)}, u32[]{:S(2)}) copy-start(f32[4096,256]{1,0:T(8,128)} %get-tuple-element.108) | copy-start | bytes 12582916
  536.2 15.7 %slice-start.2 = ((s8[8388608]{0:T(1024)(128)(4,1)}), s8[4194304]{0:T(1024)(128)(4,1)S(1)}, s32[]{:S(2)}) async-start(s8[8388608]{0:T(1024)(128)(4,1)} %bitcast.58), calls=%async_computation.16 | async-start | bytes 8388608
  543.4 8.5 slice-start
  543.4 8.5 slice-start.1
  543.4 10.3 slice-start.3
  543.4 12.7 %copy-start.10 = (f32[4096,512]{1,0:T(8,128)S(1)}, f32[4096,512]{1,0:T(8,128)}, u32[]{:S(2)}) copy-start(f32[4096,512]{1,0:T(8,128)} %get-tuple-element.22) | copy-start | bytes 25165828
  636.8 84.2 %reduce-scatter.16.cloned.1.call-start = ((), (), s32[]{:S(2)}) async-start(), calls=%async_computation.13 | async-start | bytes 1179648
  649.3 93.6 %reduce-scatter.14.cloned.1.call-start = ((), (), s32[]{:S(2)}) async-start(), calls=%async_computation.12 | async-start | bytes 81920 | tf_op jit(solution)/shard_map/reduce_scatter | solution.py:424
  682.5 205.5 %reduce-scatter.10.cloned.1.call-start = ((), (), s32[]{:S(2)}) async-start(), calls=%async_computation.10 | async-start | bytes 10485760 | tf_op jit(solution)/shard_map/reduce_scatter | solution.py:419
  701.5 1.2 copy-start.22
  701.5 335.1 %reduce-scatter.8.cloned.1.call-start = ((), (), s32[]{:S(2)}) async-start(), calls=%async_computation.9 | async-start | bytes 10485760 | tf_op jit(solution)/shard_map/reduce_scatter | solution.py:389
  713.3 1.6 copy-start.4
  713.3 2.8 copy-start.14
  713.3 3.1 copy-start.21
  713.3 9.6 copy-start.12
Sparse Core Ops, SparseCore 0:
  26.8 32.7 all-gather.6
  61.2 149.6 all-gather.4
  212.7 21.7 all-gather.10
  235.9 149.6 all-gather.8
  636.9 44.0 reduce-scatter.11
  684.9 36.0 reduce-scatter.15
  723.9 18.9 reduce-scatter.13
  745.3 142.6 reduce-scatter.9
  890.4 146.1 reduce-scatter.7

commit v2 on v1

--- a/solution.py
+++ b/solution.py
@@ -336,9 +336,13 @@
         ],
         axis=1,
     )
-    w_all = lax.all_gather(w_mine, "dp", axis=0, tiled=True)
-    w_out_rows = lax.all_gather(w_out, "dp", axis=0, tiled=True)
-    cot_all = lax.all_gather(grad_out, "tensor", axis=0, tiled=True)
+    hidden_all, w_mine, cot_mine = lax.optimization_barrier((hidden_all, w_mine, grad_out))
+    w_all = lax.all_gather(
+        jnp.concatenate([w_mine, w_out], axis=1), "dp", axis=0, tiled=True
+    )
+    w_out_rows = w_all[:, w_mine.shape[1] :]
+    w_all = w_all[:, : w_mine.shape[1]]
+    cot_all = lax.all_gather(cot_mine, "tensor", axis=0, tiled=True)
     bc_at = 2 * inner_loc
     dt_at = bc_at + maps_dim
     gain_val = w_all[:, dt_at + heads].astype(jnp.float32)
@@ -386,28 +390,25 @@
     dz_low = (d_gated * y_val * sigma_z * (1.0 + z_val * (1.0 - sigma_z))).astype(jnp.bfloat16)
     normed_gate = (gated * gate_scale * gn_gain).astype(jnp.bfloat16)
     d_gain_part = jnp.sum(d_gate_norm * gated * gate_scale, 0)
-    branch = lax.psum_scatter(
-        contract_cols(normed_gate, w_out_rows).astype(jnp.bfloat16),
-        "tensor",
-        scatter_dimension=0,
-        tiled=True,
-    ).astype(jnp.float32)
-    mixed = (hidden + branch).astype(jnp.bfloat16)
-    g_out = lax.psum_scatter(
-        contract_rows(cot_all, normed_gate).astype(jnp.bfloat16),
-        "dp",
-        scatter_dimension=0,
-        tiled=True,
-    ).astype(jnp.float32)
+    branch_part = contract_cols(normed_gate, w_out_rows).astype(jnp.bfloat16)
+    d_w_early = jnp.concatenate(
+        [
+            contract_rows(cot_all, normed_gate).astype(jnp.bfloat16),
+            contract_rows(normed_all, dz_low).astype(jnp.bfloat16),
+        ],
+        axis=1,
+    )
+    dy_low, branch_part, d_w_early = lax.optimization_barrier((dy_low, branch_part, d_w_early))
+    branch = lax.psum_scatter(branch_part, "tensor", scatter_dimension=0, tiled=True)
+    g_early = lax.psum_scatter(d_w_early, "dp", scatter_dimension=0, tiled=True)
     dxs, dmaps, dstep, d_rate_terms, dskip_rows = scan_backward(
         xs, maps, cols, rows, rates, skip_wide, dy_low, states
     )
     d_a_log = jnp.sum(d_rate_terms * step, 0) * rates
     d_skip = jnp.sum(dskip_rows[0].reshape(heads, width), 1)
     d_inner, d_bc, d_dt, d_conv_x, d_conv_bc, d_dt_bias = conv_back((dxs, dmaps, dstep))
-    d_all = jnp.concatenate(
+    d_rest = jnp.concatenate(
         [
-            dz_low,
             d_inner.astype(jnp.bfloat16),
             d_bc.astype(jnp.bfloat16),
             d_dt.astype(jnp.bfloat16),
@@ -415,23 +416,30 @@
         ],
         axis=1,
     )
-    term = contract_cols(d_all, w_all).astype(jnp.bfloat16)
+    term = (
+        contract_cols(dz_low, w_all[:, :inner_loc]) + contract_cols(d_rest, w_all[:, inner_loc:])
+    ).astype(jnp.bfloat16)
+    term, branch, g_early, d_rest = lax.optimization_barrier((term, branch, g_early, d_rest))
+    mixed = (hidden + branch.astype(jnp.float32)).astype(jnp.bfloat16)
+    g_out = g_early[:, :inner_loc].astype(jnp.float32)
     d_normed = lax.psum_scatter(term, "tensor", scatter_dimension=0, tiled=True).astype(
         jnp.float32
     )
-    d_w = contract_rows(normed_all, d_all).astype(jnp.bfloat16)
-    g_all = lax.psum_scatter(d_w, "dp", scatter_dimension=0, tiled=True)
+    d_w = contract_rows(normed_all, d_rest).astype(jnp.bfloat16)
+    g_rest = lax.psum_scatter(d_w, "dp", scatter_dimension=0, tiled=True)
     g_bc = lax.psum_scatter(
-        g_all[:, bc_at:dt_at], "tensor", scatter_dimension=0, tiled=True
+        g_rest[:, inner_loc : inner_loc + maps_dim], "tensor", scatter_dimension=0, tiled=True
     ).astype(jnp.float32)
-    g_zx = g_all[:, :bc_at].astype(jnp.float32).reshape(rows_loc, 2, inner_loc)
-    g_dt = g_all[:, dt_at : dt_at + heads].astype(jnp.float32)
+    g_zx = (
+        jnp.stack([g_early[:, inner_loc:], g_rest[:, :inner_loc]], axis=1).astype(jnp.float32)
+    )
+    g_dt = g_rest[:, inner_loc + maps_dim : inner_loc + maps_dim + heads].astype(jnp.float32)
     pre_grad = d_normed * gain_val
     d_hidden = pre_scale * pre_grad - hidden * pre_scale**3 * jnp.mean(
         pre_grad * hidden, -1, keepdims=True
     )
     grad_input = grad_out.astype(jnp.float32) + d_hidden
-    d_norm_gain = jnp.sum(d_normed * hidden * pre_scale, 0)
+    d_norm_gain = jnp.sum(term.astype(jnp.float32) * hidden_val * scale_all, 0)
     sums_all = lax.psum(
         (
             spread_part(d_conv_x, 1, tensor_count, tensor_rank),

time: 1060 us -> 872 us (0.82)
  waiting for transfers between devices: 556 us -> 371 us
  other arithmetic: 114 us -> 134 us
  local copies, waits for them, and re-layouts: 46 us -> 26.3 us
    reduce_scatter x3 -> x1, waiting for transfers between devices: 145 us -> 0.02 us  [body(): lax.psum_scatter(branch_part, 'tensor', scatter_dimension=0, tiled=True)]
    reduce_scatter x1, waiting for transfers between devices: 144 us -> 107 us  [body(): lax.psum_scatter(term, 'tensor', scatter_dimension=0, tiled=True)]
    unnamed x10 -> x11, waiting for transfers between devices: 6.52 us -> 40.8 us
    all_gather x3 -> x2, waiting for transfers between devices: 110 us -> 89.4 us  [the longest x1 62.4 us: body(): cot_all = lax.all_gather(cot_mine, 'tensor', axis=0, tiled=True)]
    concatenate x1, local copies, waits for them, and re-layouts: 17 us -> 0.08 us  [body(): jnp.concatenate([d_inner.astype(jnp.bfloat16), d_bc.astype(jnp.bfloat16),...]
    all_gather x1, waiting for transfers between devices: 151 us -> 134 us  [body(): hidden_all = lax.all_gather(hidden_in, 'tensor', axis=0, tiled=True)]
    reduce_sum x2, other arithmetic: 17.6 us -> 30.7 us  [causal_conv(): weights[offset]]
    dot_general x2 -> x3, matrix products: 29.5 us -> 33.8 us  [contract_cols(): lax.dot_general(left, right, (((1,), (1,)), ((), ())), preferred_element_...]
  transfers between devices with their start and end apart: 9 -> 8, of which waited for: 8 -> 5; matrix products, arithmetic and copies ran while one was open for 10% -> 20% of each run, Pallas kernels for 4% -> 16%
where the time goes in v2:
time: 872 us; the launch traced here: 867 us
  waiting for transfers between devices  371 us (43%)
  Pallas kernels  143 us (16%)
  other arithmetic  134 us (15%)
  matrix products  105 us (12%)
  blocking collectives  73.1 us (8%)
  local copies, waits for them, and re-layouts  26.3 us (3%)
  between operations  15.2 us (2%)
    all_gather x1, waiting for transfers between devices, body(): hidden_all = lax.all_gather(hidden_in, 'tensor', axis=0, tiled=True)  134 us
    reduce_scatter x1, waiting for transfers between devices, body(): lax.psum_scatter(term, 'tensor', scatter_dimension=0, tiled=True)  107 us
    pallas_call x1, Pallas kernels, scan_backward(): pl.pallas_call(backward_kernel, grid=(blocks,), in_specs=block_specs(leng...  97.8 us
    all_gather x1, waiting for transfers between devices, body(): cot_all = lax.all_gather(cot_mine, 'tensor', axis=0, tiled=True)  62.4 us
    pallas_call x1, Pallas kernels, scan_forward(): pl.pallas_call(forward_kernel, grid=(blocks,), in_specs=block_specs(lengt...  44.8 us
    psum x1, blocking collectives, body(): lax.psum((spread_part(d_conv_x, 1, tensor_count, tensor_rank), d_conv_bc,...  42.1 us
    unnamed x11, waiting for transfers between devices  40.8 us
    dot_general x3, matrix products, contract_cols(): lax.dot_general(left, right, (((1,), (1,)), ((), ())), preferred_element_...  33.8 us
  transfers between devices with their start and end apart: 8, of which 5 were waited for; matrix products, arithmetic and copies ran while one was open for 20% of the time, Pallas kernels for 16%

profile of v2, /device:TPU:0, one launch (start us, length us, event | category | flops | bytes accessed | tf_op | source)
XLA Modules:
  0.0 867.5 jit_solution(17857571386480070838)
XLA Ops:
  7.3 0.7 all-gather.4.cloned.1.call-update
  8.0 0.8 copy.110
  8.8 0.7 fusion.44
  9.5 15.0 %all_gather.13 = bf16[128,384]{1,0:T(8,128)(2,1)S(1)} all-gather(bf16[32,384]{1,0:T(8,128)(2,1)S(1)} %fusion.44), channel_id=1, replica_groups=mesh['dp'=8,'tensor'=4] {'tensor'}, dimensions={0}, use_global_device_ids=true | all-gather | bytes 122880 | tf_op jit(solution)/shard_map/all_gather | solution.py:329
  24.8 1.2 copy.98
  26.0 1.0 copy.84
  27.0 0.7 pad_maximum_fusion.2
  27.7 134.3 %all-gather.4.cloned.1.call-done = bf16[4096,1024]{1,0:T(8,128)(2,1)} async-done(((bf16[1024,1024]{1,0:T(8,128)(2,1)}), bf16[4096,1024]{1,0:T(8,128)(2,1)}) %all-gather.4.cloned.1.call-update) | async-done | bytes 8388624 | tf_op jit(solution)/shard_map/all_gather | solution.py:327
  162.0 0.8 pad_maximum_fusion.1
  163.4 1.4 reduce.7
  165.6 0.7 copy.87
  166.8 5.3 fusion
  172.1 27.0 %all-gather.6.cloned.1.call-done = bf16[1024,1920]{0,1:T(8,128)(2,1)} async-done(((bf16[128,1920]{0,1:T(8,128)(2,1)}), bf16[1024,1920]{0,1:T(8,128)(2,1)}) %all-gather.6.cloned.1.call-update) | async-done | bytes 3932176 | tf_op jit(solution)/shard_map/all_gather | solution.py:340
  199.2 0.7 slice_convert_fusion.1
  199.9 7.5 fusion.41
  207.4 2.6 slice.176
  210.0 1.2 fusion.52
  211.1 0.9 copy-done.4
  212.0 1.3 copy-done.5
  213.3 2.0 maximum_maximum_fusion.1
  215.3 2.2 copy.88.rows_ref
  217.5 2.4 fusion.72.cols_ref
  220.3 6.0 fusion.28
  226.3 7.4 fusion.33
  233.7 9.5 %fusion.18 = (f32[4096,512]{1,0:T(8,128)}, f32[4096,512]{1,0:T(8,128)}) fusion(f32[4096,512]{1,0:T(8,128)S(1)} %fusion.33, f32[512]{0:T(512)S(1)} %bitcast.79, pred[4096]{0:T(1024)(128)(4,1)S(1)} %get-tuple-element.158, f32[512]{0:T(512)S(1)} %bitcast.81, pred[4096]{0:T(1024)(128)(4,1)S(1)} %get-tuple-element.157, f32[512]{0:T(512)S(1)} %bitcast.75, ...), kind=kLoop, calls=%fused_computation.44 | loop fusion | flops 31457280 | bytes 25188352 | tf_op jit(solution)/shard_map/jvp(jit(silu))/mul | solution.py:279
  243.3 44.8 %scan_forward.1 = (bf16[4096,512]{1,0:T(8,128)(2,1)}, f32[16,512,128]{2,1,0:T(8,128)}) custom-call(f32[4096,512]{1,0:T(8,128)} %get-tuple-element.129.x_ref, f32[4096,256]{1,0:T(8,128)} %get-tuple-element.127.bc_ref, f32[4096,16]{1,0:T(8,128)S(1)} %fusion.72.cols_ref, f32[16,4096]{1,0:T(8,128)S(1)} %copy.88.rows_ref, ...), custom_call_target="tpu_custom_call" | custom-call | flops 12000000000 | bytes 24000000 | tf_op jit(solution)/shard_map/scan_forward/pallas_call | solution.py:205
  288.0 62.4 %all-gather.8.cloned.1.call-done = bf16[4096,1024]{1,0:T(8,128)(2,1)} async-done(((bf16[1024,1024]{1,0:T(8,128)(2,1)}), bf16[4096,1024]{1,0:T(8,128)(2,1)}) %all-gather.8.cloned.1.call-update) | async-done | bytes 8388624 | tf_op jit(solution)/shard_map/all_gather | solution.py:345
  350.4 8.1 fusion.36
  358.6 15.2 %multiply_reduce_fusion.6 = (f32[4096]{0:T(1024)S(1)}, f32[4096]{0:T(1024)S(1)}, bf16[4096,512]{1,0:T(8,128)(2,1)}) fusion(bf16[4096,512]{1,0:T(8,128)(2,1)S(1)} %copy-done.11, f32[4096,512]{1,0:T(8,128)S(1)} %fusion.36, f32[512]{0:T(512)S(1)} %convert_element_type.111, bf16[1024,1920]{0,1:T(8,128)(2,1)} %all-gather.6.cloned.1.call-done, ...), kind=kOutput, calls=%fused_computation.42 | convolution fusion | flops 4338999296 | bytes 26269696 | tf_op jit(solution)/shard_map/dot_general | solution.py:354
  373.8 16.1 %psum.56 = f32[2,4096]{1,0:T(2,128)S(1)} all-reduce(f32[2,4096]{1,0:T(2,128)S(1)} %pad_maximum_fusion.3), channel_id=1, replica_groups=mesh['dp'=8,'tensor'=4] {'tensor'}, use_global_device_ids=true, to_apply=%region_3.4 | all-reduce | flops 8192 | bytes 65536 | tf_op jit(solution)/shard_map/psum | solution.py:383
  389.9 12.6 %fusion.16 = (bf16[4096,512]{1,0:T(8,128)(2,1)}, bf16[4096,512]{1,0:T(8,128)(2,1)S(1)}, f32[512]{0:T(512)}) fusion(bf16[4096,512]{1,0:T(8,128)(2,1)} %get-tuple-element.168, f32[4096]{0:T(1024)S(1)} %bitcast.65, f32[4096]{0:T(1024)S(1)} %multiply_multiply_fusion, f32[4096,512]{1,0:T(8,128)} %copy-done.7, f32[512]{0:T(512)S(1)} %convert_element_type.111, ...), kind=kLoop, calls=%fused_computation.26 | loop fusion | flops 52428288 | bytes 25219072 | tf_op jit(solution)/shard_map/convert_element_type | solution.py:389
  402.5 9.9 %convolution_convert_fusion.3 = bf16[1024,512]{0,1:T(8,128)(2,1)S(1)} fusion(bf16[4096,512]{1,0:T(8,128)(2,1)S(1)} %get-tuple-element.132, bf16[4096,1024]{1,0:T(8,128)(2,1)} %all-gather.4.cloned.1.call-done, f32[1024]{0:T(1024)S(1)} %bitcast.71, f32[4096]{0:T(1024)S(1)} %add_rsqrt_fusion), kind=kOutput, calls=%fused_computation.97 | convolution fusion | flops 4312268800 | bytes 13651968 | tf_op jit(solution)/shard_map/dot_general | solution.py:285
  412.5 8.7 convolution_convert_fusion.4
  421.3 9.8 %convolution_convert_fusion = bf16[4096,1024]{1,0:T(8,128)(2,1)} fusion(bf16[1024,1920]{0,1:T(8,128)(2,1)} %all-gather.6.cloned.1.call-done, f32[4096]{0:T(1024)S(1)} %bitcast.64, f32[512]{0:T(512)S(1)} %convert_element_type.111, bf16[4096,512]{1,0:T(8,128)(2,1)S(1)} %copy-done.13, bf16[4096,512]{1,0:T(8,128)(2,1)S(1)} %copy-done.12), kind=kOutput, calls=%fused_computation.49 | convolution fusion | flops 4320133120 | bytes 17844224 | tf_op jit(solution)/shard_map/dot_general | solution.py:291
  431.1 2.5 copy.99
  434.4 97.8 %scan_backward.1 = (f32[4096,512]{1,0:T(8,128)}, f32[4096,256]{1,0:T(8,128)}, f32[4096,8]{1,0:T(8,128)S(1)}, f32[4096,8]{1,0:T(8,128)S(1)}, f32[8,512]{1,0:T(8,128)S(1)}) custom-call(f32[4096,512]{1,0:T(8,128)} %get-tuple-element.129.x_ref, f32[4096,256]{1,0:T(8,128)} %get-tuple-element.127.bc_ref, f32[4096,16]{1,0:T(8,128)} %copy-done, ...), custom_call_target="tpu_custom_call" | custom-call | flops 30000001024 | bytes 40000000 | tf_op jit(solution)/shard_map/scan_backward/pallas_call | solution.py:232
  532.2 7.3 multiply_reduce_fusion.10
  539.6 5.0 broadcast_multiply_fusion.1
  544.6 6.2 fusion.27
  550.8 23.4 %multiply_reduce_fusion.4 = (f32[512]{0:T(512)S(1)}, f32[512]{0:T(512)S(1)}, f32[512]{0:T(512)S(1)}, f32[512]{0:T(512)S(1)}, f32[512]{0:T(512)S(1)}, /*index=5*/f32[4096,512]{1,0:T(8,128)S(1)}) fusion(f32[4096,512]{1,0:T(8,128)} %copy-done.3, pred[4096]{0:T(1024)(128)(4,1)S(1)} %get-tuple-element.156, pred[4096]{0:T(1024)(128)(4,1)S(1)} %get-tuple-element.157, ...), kind=kLoop, calls=%fused_computation.35 | loop fusion | flops 44037632 | bytes 33576960 | tf_op jit(solution)/shard_map/transpose(jvp())/reduce_sum | solution.py:23
  574.3 11.4 %broadcast_multiply_fusion = (f32[4096,512]{1,0:T(8,128)}, f32[4096,512]{1,0:T(8,128)}, f32[4096,512]{1,0:T(8,128)}, f32[4096,512]{1,0:T(8,128)}) fusion(f32[4096,512]{1,0:T(8,128)S(1)} %get-tuple-element.126, f32[512]{0:T(512)S(1)} %bitcast.80, f32[512]{0:T(512)S(1)} %bitcast.78, pred[4096]{0:T(1024)(128)(4,1)S(1)} %get-tuple-element.156, ...), kind=kLoop, calls=%fused_computation.86 | loop fusion | flops 14680064 | bytes 41963520 | tf_op jit(solution)/shard_map/transpose(jvp())/mul | solution.py:23
  585.7 12.2 %fusion.17 = bf16[4096,512]{1,0:T(8,128)(2,1)S(1)} fusion(f32[4096,512]{1,0:T(8,128)} %get-tuple-element.135, f32[4096,512]{1,0:T(8,128)} %get-tuple-element.136, f32[4096,512]{1,0:T(8,128)} %get-tuple-element.137, f32[4096,512]{1,0:T(8,128)} %get-tuple-element.134), kind=kLoop, calls=%fused_computation.28 | loop fusion | flops 8388608 | bytes 37748736 | tf_op jit(solution)/shard_map/convert.2
  598.0 3.7 fusion.60
  601.7 3.9 maximum_maximum_fusion
  606.0 9.5 %fusion.38 = f32[4096,1024]{1,0:T(8,128)} fusion(bf16[4096,512]{1,0:T(8,128)(2,1)S(1)} %copy-done.10, bf16[1024,1920]{0,1:T(8,128)(2,1)} %all-gather.6.cloned.1.call-done), kind=kOutput, calls=%fused_computation.104 | convolution fusion | flops 4294967296 | bytes 22020096 | tf_op jit(solution)/shard_map/dot_general | solution.py:291
  615.5 14.5 %add_convert_fusion = bf16[4096,1024]{1,0:T(8,128)(2,1)} fusion(f32[4096,1024]{1,0:T(8,128)} %fusion.38, bf16[4096,896]{1,0:T(8,128)(2,1)S(1)} %copy-done.8, bf16[1024,1920]{0,1:T(8,128)(2,1)} %all-gather.6.cloned.1.call-done), kind=kOutput, calls=%fused_computation.8 | convolution fusion | flops 7524581376 | bytes 34340864 | tf_op jit(solution)/shard_map/dot_general | solution.py:291
  630.0 1.1 copy.100
  631.2 14.5 %convolution_convert_fusion.2 = bf16[1024,896]{1,0:T(8,128)(2,1)} fusion(bf16[4096,896]{1,0:T(8,128)(2,1)} %maximum_maximum_fusion, bf16[4096,1024]{1,0:T(8,128)(2,1)} %all-gather.4.cloned.1.call-done, f32[1024]{0:T(1024)S(1)} %bitcast.72, f32[4096]{0:T(1024)S(1)} %copy-done.16), kind=kOutput, calls=%fused_computation.96 | convolution fusion | flops 7533887488 | bytes 17584128 | tf_op jit(solution)/shard_map/dot_general | solution.py:285
  645.8 38.9 %reduce-scatter.18.cloned.1.call-done = bf16[128,896]{1,0:T(8,128)(2,1)} async-done(((bf16[1024,896]{1,0:T(8,128)(2,1)}), bf16[128,896]{1,0:T(8,128)(2,1)}) %reduce-scatter.18.cloned.1.call-update) | async-done | bytes 229392
  684.6 1.5 slice.186
  686.2 0.7 reduce-scatter.14.cloned.1.call-update
  688.0 7.7 fusion.4
  695.8 42.1 %all-reduce.22 = (f32[1024]{0:T(1024)S(1)}, f32[5,2048]{1,0:T(8,128)S(1)}, f32[5,256]{1,0:T(8,128)}, f32[32]{0:T(128)S(1)}, f32[32]{0:T(128)S(1)}, /*index=5*/f32[32]{0:T(128)S(1)}, f32[2048]{0:T(1024)S(1)}) all-reduce(f32[1024]{0:T(1024)S(1)} %fusion.4, ...), channel_id=1, replica_groups=mesh['dp'=8,'tensor'=4] {'dp','tensor'}, use_global_device_ids=true, to_apply=%region_10.11 | all-reduce | flops 14688 | bytes 117504 | tf_op jit(solution)/shard_map/psum | solution.py:443
  737.8 0.7 dynamic_slice.23
  738.5 0.6 dynamic_slice.20
  740.3 0.8 copy.96
  741.7 0.6 constant_dynamic-slice_fusion
  742.5 1.0 copy.94
  743.5 0.6 convert_element_type.128
  744.2 0.8 copy.104
  745.0 0.7 copy.95
  745.7 106.6 %reduce-scatter.14.cloned.1.call-done = bf16[1024,1024]{1,0:T(8,128)(2,1)} async-done(((bf16[4096,1024]{1,0:T(8,128)(2,1)}), bf16[1024,1024]{1,0:T(8,128)(2,1)}) %reduce-scatter.14.cloned.1.call-update) | async-done | bytes 2097168 | tf_op jit(solution)/shard_map/reduce_scatter | solution.py:425
  852.3 2.6 fusion.22
  855.0 5.4 fusion.25
  (163 shorter events, 7.2 us)
Async XLA Ops:
  7.2 158.3 %copy-start.14 = (s32[1,4096]{1,0:T(1,128)S(1)}, s32[1,4096]{1,0:T(1,128)}, u32[]{:S(2)}) copy-start(s32[1,4096]{1,0:T(1,128)} %param.15) | copy-start | bytes 49156
  7.2 159.1 %copy-start.42 = (f32[8]{0:T(128)S(1)}, f32[8]{0:T(128)}, u32[]{:S(2)}) copy-start(f32[8]{0:T(128)} %param.22) | copy-start | bytes 100
  7.2 159.2 %copy-start.41 = (f32[8]{0:T(128)S(1)}, f32[8]{0:T(128)}, u32[]{:S(2)}) copy-start(f32[8]{0:T(128)} %param.24) | copy-start | bytes 100
  7.2 159.3 %copy-start.40 = (bf16[512]{0:T(512)(128)(2,1)S(1)}, bf16[512]{0:T(512)(128)(2,1)}, u32[]{:S(2)}) copy-start(bf16[512]{0:T(512)(128)(2,1)} %param.25) | copy-start | bytes 3076
  7.2 159.4 %copy-start.37 = (f32[5,256]{1,0:T(8,128)S(1)}, f32[5,256]{1,0:T(8,128)}, u32[]{:S(2)}) copy-start(f32[5,256]{1,0:T(8,128)} %param.21) | copy-start | bytes 15364
  7.2 159.4 %copy-start.36 = (f32[5,512]{1,0:T(8,128)S(1)}, f32[5,512]{1,0:T(8,128)}, u32[]{:S(2)}) copy-start(f32[5,512]{1,0:T(8,128)} %param.20) | copy-start | bytes 30724
  7.2 154.8 %all-gather.4.cloned.1.call-start = ((), (), s32[]{:S(2)}) async-start(), calls=%async_computation.5 | async-start | bytes 10485760 | tf_op jit(solution)/shard_map/all_gather | solution.py:327
  8.0 191.2 %all-gather.6.cloned.1.call-start = ((), (), s32[]{:S(2)}) async-start(), calls=%async_computation.6 | async-start | bytes 4423680 | tf_op jit(solution)/shard_map/all_gather | solution.py:340
  162.9 187.5 %all-gather.8.cloned.1.call-start = ((), (), s32[]{:S(2)}) async-start(), calls=%async_computation.7 | async-start | bytes 10485760 | tf_op jit(solution)/shard_map/all_gather | solution.py:345
  165.5 464.5 %reduce-scatter.16.cloned.1.call-start = ((), (), s32[]{:S(2)}) async-start(), calls=%async_computation.10 | async-start | bytes 2359296
  166.6 53.2 %copy-start.27 = (f32[1,256]{1,0:T(1,128)}, f32[1,256]{1,0:T(1,128)S(1)}, u32[]{:S(2)}) copy-start(f32[1,256]{1,0:T(1,128)S(1)} %get-tuple-element.160) | copy-start | bytes 3076
  166.6 53.2 %copy-start.29 = (f32[1,256]{1,0:T(1,128)}, f32[1,256]{1,0:T(1,128)S(1)}, u32[]{:S(2)}) copy-start(f32[1,256]{1,0:T(1,128)S(1)} %get-tuple-element.161) | copy-start | bytes 3076
  166.6 53.2 %copy-start.31 = (f32[1,256]{1,0:T(1,128)}, f32[1,256]{1,0:T(1,128)S(1)}, u32[]{:S(2)}) copy-start(f32[1,256]{1,0:T(1,128)S(1)} %get-tuple-element.162) | copy-start | bytes 3076
  166.7 53.2 %copy-start.33 = (f32[1,256]{1,0:T(1,128)}, f32[1,256]{1,0:T(1,128)S(1)}, u32[]{:S(2)}) copy-start(f32[1,256]{1,0:T(1,128)S(1)} %get-tuple-element.163) | copy-start | bytes 3076
  166.7 67.0 %copy-start.19 = (f32[1,512]{1,0:T(1,128)}, f32[1,512]{1,0:T(1,128)S(1)}, u32[]{:S(2)}) copy-start(f32[1,512]{1,0:T(1,128)S(1)} %get-tuple-element.152) | copy-start | bytes 6148
  166.7 67.0 %copy-start.21 = (f32[1,512]{1,0:T(1,128)}, f32[1,512]{1,0:T(1,128)S(1)}, u32[]{:S(2)}) copy-start(f32[1,512]{1,0:T(1,128)S(1)} %get-tuple-element.153) | copy-start | bytes 6148
  166.7 67.0 %copy-start.23 = (f32[1,512]{1,0:T(1,128)}, f32[1,512]{1,0:T(1,128)S(1)}, u32[]{:S(2)}) copy-start(f32[1,512]{1,0:T(1,128)S(1)} %get-tuple-element.154) | copy-start | bytes 6148
  166.7 67.0 %copy-start.25 = (f32[1,512]{1,0:T(1,128)}, f32[1,512]{1,0:T(1,128)S(1)}, u32[]{:S(2)}) copy-start(f32[1,512]{1,0:T(1,128)S(1)} %get-tuple-element.155) | copy-start | bytes 6148
  172.1 230.4 %copy-start.15 = (f32[4096]{0:T(1024)}, f32[4096]{0:T(1024)S(1)}, u32[]{:S(2)}) copy-start(f32[4096]{0:T(1024)S(1)} %add_rsqrt_fusion) | copy-start | bytes 49156
  199.9 202.6 %copy-start.17 = (f32[1024,1]{0,1:T(1,128)}, f32[1024,1]{0,1:T(1,128)S(1)}, u32[]{:S(2)}) copy-start(f32[1024,1]{0,1:T(1,128)S(1)} %slice_convert_fusion.1) | copy-start | bytes 12292
  207.4 4.6 copy-start.4
  207.4 2.6 copy-start.38
  212.0 1.3 copy-start.5
  217.5 2.8 copy-start.1
  219.8 23.4 %copy-start = (f32[4096,16]{1,0:T(8,128)}, f32[4096,16]{1,0:T(8,128)S(1)}, u32[]{:S(2)}) copy-start(f32[4096,16]{1,0:T(8,128)S(1)} %fusion.72.cols_ref) | copy-start | bytes 786436
  233.7 9.6 %copy-start.3 = (f32[4096,512]{1,0:T(8,128)}, f32[4096,512]{1,0:T(8,128)S(1)}, u32[]{:S(2)}) copy-start(f32[4096,512]{1,0:T(8,128)S(1)} %fusion.33) | copy-start | bytes 25165828
  350.4 8.2 copy-start.11
  358.5 15.2 %copy-start.7 = (f32[4096,512]{1,0:T(8,128)}, f32[4096,512]{1,0:T(8,128)S(1)}, u32[]{:S(2)}) copy-start(f32[4096,512]{1,0:T(8,128)S(1)} %fusion.36) | copy-start | bytes 25165828
  402.5 9.9 %copy-start.9 = (bf16[4096,512]{1,0:T(8,128)(2,1)}, bf16[4096,512]{1,0:T(8,128)(2,1)S(1)}, u32[]{:S(2)}) copy-start(bf16[4096,512]{1,0:T(8,128)(2,1)S(1)} %get-tuple-element.132) | copy-start | bytes 12582916
  402.5 9.9 %copy-start.12 = (bf16[4096,512]{1,0:T(8,128)(2,1)S(1)}, bf16[4096,512]{1,0:T(8,128)(2,1)}, u32[]{:S(2)}) copy-start(bf16[4096,512]{1,0:T(8,128)(2,1)} %get-tuple-element.32) | copy-start | bytes 12582916
  402.5 10.0 %copy-start.13 = (bf16[4096,512]{1,0:T(8,128)(2,1)S(1)}, bf16[4096,512]{1,0:T(8,128)(2,1)}, u32[]{:S(2)}) copy-start(bf16[4096,512]{1,0:T(8,128)(2,1)} %get-tuple-element.168) | copy-start | bytes 12582916
  433.7 197.4 %reduce-scatter.12.cloned.1.call-start = ((), (), s32[]{:S(2)}) async-start(), calls=%async_computation.8 | async-start | bytes 10485760 | tf_op jit(solution)/shard_map/reduce_scatter | solution.py:402
  434.3 250.3 %reduce-scatter.18.cloned.1.call-start = ((), (), s32[]{:S(2)}) async-start(), calls=%async_computation.11 | async-start | bytes 2064384
  434.3 97.8 %copy-start.2 = (f32[4096,256]{1,0:T(8,128)S(1)}, f32[4096,256]{1,0:T(8,128)}, u32[]{:S(2)}) copy-start(f32[4096,256]{1,0:T(8,128)} %slice.176) | copy-start | bytes 12582916
  532.2 7.4 copy-start.28
  532.2 7.4 copy-start.30
  532.2 7.4 copy-start.32
  532.2 7.4 copy-start.34
  550.8 23.5 %copy-start.20 = (f32[1,512]{1,0:T(1,128)S(1)}, f32[1,512]{1,0:T(1,128)}, u32[]{:S(2)}) copy-start(f32[1,512]{1,0:T(1,128)} %copy-done.19) | copy-start | bytes 6148
  550.8 23.5 %copy-start.22 = (f32[1,512]{1,0:T(1,128)S(1)}, f32[1,512]{1,0:T(1,128)}, u32[]{:S(2)}) copy-start(f32[1,512]{1,0:T(1,128)} %copy-done.21) | copy-start | bytes 6148
  550.8 23.5 %copy-start.24 = (f32[1,512]{1,0:T(1,128)S(1)}, f32[1,512]{1,0:T(1,128)}, u32[]{:S(2)}) copy-start(f32[1,512]{1,0:T(1,128)} %copy-done.23) | copy-start | bytes 6148
  550.8 23.5 %copy-start.26 = (f32[1,512]{1,0:T(1,128)S(1)}, f32[1,512]{1,0:T(1,128)}, u32[]{:S(2)}) copy-start(f32[1,512]{1,0:T(1,128)} %copy-done.25) | copy-start | bytes 6148
  585.7 12.3 %copy-start.39 = (f32[8]{0:T(128)S(1)}, f32[8]{0:T(128)}, u32[]{:S(2)}) copy-start(f32[8]{0:T(128)} %param.23) | copy-start | bytes 100
  601.7 4.3 copy-start.10
  606.0 9.5 %copy-start.8 = (bf16[4096,896]{1,0:T(8,128)(2,1)S(1)}, bf16[4096,896]{1,0:T(8,128)(2,1)}, u32[]{:S(2)}) copy-start(bf16[4096,896]{1,0:T(8,128)(2,1)} %maximum_maximum_fusion) | copy-start | bytes 22020100
  615.5 15.7 %copy-start.16 = (f32[4096]{0:T(1024)S(1)}, f32[4096]{0:T(1024)}, u32[]{:S(2)}) copy-start(f32[4096]{0:T(1024)} %copy-done.15) | copy-start | bytes 49156
  615.5 15.7 %copy-start.18 = (f32[1024,1]{0,1:T(1,128)S(1)}, f32[1024,1]{0,1:T(1,128)}, u32[]{:S(2)}) copy-start(f32[1024,1]{0,1:T(1,128)} %copy-done.17) | copy-start | bytes 12292
  645.7 41.9 %copy-start.35 = (f32[512]{0:T(512)S(1)}, f32[512]{0:T(512)}, u32[]{:S(2)}) copy-start(f32[512]{0:T(512)} %get-tuple-element.133) | copy-start | bytes 6148
  645.7 42.2 %copy-start.43 = (f32[8]{0:T(128)S(1)}, f32[8]{0:T(128)}, u32[]{:S(2)}) copy-start(f32[8]{0:T(128)} %param.22) | copy-start | bytes 100
  645.7 98.5 %reduce-scatter.20.cloned.1.call-start = ((), (), s32[]{:S(2)}) async-start(), calls=%async_computation.12 | async-start | bytes 81920
  686.1 166.2 %reduce-scatter.14.cloned.1.call-start = ((), (), s32[]{:S(2)}) async-start(), calls=%async_computation.9 | async-start | bytes 10485760 | tf_op jit(solution)/shard_map/reduce_scatter | solution.py:425
  688.0 54.3 %slice-start = ((bf16[128,896]{1,0:T(8,128)(2,1)}), bf16[128,512]{1,0:T(8,128)(2,1)S(1)}, s32[]{:S(2)}) async-start(bf16[128,896]{1,0:T(8,128)(2,1)} %reduce-scatter.18.cloned.1.call-done), calls=%async_computation.13 | async-start | bytes 262144 | tf_op jit(solution)/shard_map/slice | solution.py:434
  688.0 55.5 %slice-start.1 = ((bf16[128,896]{1,0:T(8,128)(2,1)}), bf16[128,8]{1,0:T(8,128)(2,1)S(1)}, s32[]{:S(2)}) async-start(bf16[128,896]{1,0:T(8,128)(2,1)} %reduce-scatter.18.cloned.1.call-done), calls=%async_computation.14 | async-start | bytes 65536 | tf_op jit(solution)/shard_map/slice | solution.py:436
  688.0 164.3 %copy-start.6 = (bf16[1024,1024]{1,0:T(8,128)(2,1)S(1)}, bf16[1024,1024]{1,0:T(8,128)(2,1)}, u32[]{:S(2)}) copy-start(bf16[1024,1024]{1,0:T(8,128)(2,1)} %param.14) | copy-start | bytes 6291460
Sparse Core Ops, SparseCore 0:
  9.6 152.3 all-gather.3
  164.5 34.6 all-gather.5
  200.7 149.6 all-gather.7
  433.8 40.3 reduce-scatter.15
  476.6 144.4 reduce-scatter.11
  645.8 38.7 reduce-scatter.17
  687.5 18.9 reduce-scatter.19
  708.9 143.3 reduce-scatter.13
